TPU v7x, 32 devices: a whole 2x2x4 slice. The times are simulated.
32 devices in a mesh: section: 2 (over core), fsdp: 4 (over y, x), replica: 4 (over z).
Axes of the slice: x: 2, y: 2, z: 4, core: 2. Of those that a mesh axis runs over, the one named last changes fastest.
Arguments:
- inputs: bfloat16 [24576, 576], P(('fsdp', 'replica')), may hold values from -6 to 6
- cotangent: bfloat16 [24576, 576], P(('fsdp', 'replica')), may hold values from -6 to 6
- seq_lengths: int32 [32, 4], P(('fsdp', 'replica')), may hold values from 1 to 640, 768 in all within a row
- attn_gain: bfloat16 [2, 576], P('section', 'fsdp'), may hold values from 0.5 to 1.5
- w_query: bfloat16 [2, 576, 576], P('section', 'fsdp'), may hold values from -0.25 to 0.25
- key_value_weight: bfloat16 [2, 576, 384], P('section', 'fsdp'), may hold values from -0.25 to 0.25
- w_out: bfloat16 [2, 576, 576], P('section', 'fsdp'), may hold values from -1.5 to 1.5
- ffn_gain: bfloat16 [2, 576], P('section', 'fsdp'), may hold values from 0.5 to 1.5
- w_gateup: bfloat16 [2, 576, 3072], P('section', 'fsdp'), may hold values from -0.25 to 0.25
- w_down: bfloat16 [2, 1536, 576], P('section', 'fsdp'), may hold values from -0.15625 to 0.15625
Outputs:
- activations: bfloat16 [2, 24576, 576], P('section', ('fsdp', 'replica'))
- input_grads: float32 [2, 24576, 576], P('section', ('fsdp', 'replica'))
- grad_attn_gain: float32 [2, 576], P('section', 'fsdp')
- grad_query: float32 [2, 576, 576], P('section', 'fsdp')
- grad_keyval: float32 [2, 576, 384], P('section', 'fsdp')
- grad_out: float32 [2, 576, 576], P('section', 'fsdp')
- grad_ffn_gain: float32 [2, 576], P('section', 'fsdp')
- grad_gateup: float32 [2, 576, 3072], P('section', 'fsdp')
- grad_down: float32 [2, 1536, 576], P('section', 'fsdp')
Inputs may be any that keep to these rules, and one draw needn't show every extreme that they name: `seq_lengths`: each row holds the lengths of the 4 sequences of one micro-batch in order; a row sums to 768 and its largest entry is exactly 640.
All inputs are finite; a program needn't handle non-finite values.
Results may differ from a plain program's by a relative error of at most 0.023.
Values may be sent and summed in bfloat16 or wider, within the bound.
A program may use at most 256 MiB of HBM per device.

v0:
```python
import jax
import jax.numpy as jnp
from jax import lax
from jax.sharding import PartitionSpec as P

QUERY_HEADS = 9
KEY_VALUE_HEADS = 3
HEAD_SIZE = 64
FF = 1536
MICRO = 2


EPS = 1e-05
ROPE_BASE = 100000.0


def shifted_2(value, axis, steps):
    count = lax.axis_size(axis)
    first, last = (max(0, -steps), min(count, count - steps))
    return lax.ppermute(value, axis, [(source, source + steps) for source in range(first, last)])


def positions(lengths, token_count):
    ends = jnp.cumsum(lengths)
    index = jnp.arange(token_count, dtype=jnp.int32)
    after = index[:, None] >= ends[None, :]
    segment = jnp.sum(after.astype(jnp.int32), 1)
    place = index - jnp.sum(jnp.where(after, lengths[None, :], 0), 1)
    return (segment, place)


def rope_tables(place, width):
    half = width // 2
    freq = ROPE_BASE ** (-(jnp.arange(half, dtype=jnp.float32) * 2.0 / width))
    angle = place.astype(jnp.float32)[:, None] * freq[None, :]
    angle = jnp.concatenate([angle, angle], 1)
    return (jnp.cos(angle)[:, None, :], jnp.sin(angle)[:, None, :])


def rotary_apply(value_rows, cosine_table, sine_table):
    half = value_rows.shape[-1] // 2
    turned = jnp.concatenate([-value_rows[..., half:], value_rows[..., :half]], -1)
    return value_rows * cosine_table + turned * sine_table


def rotary_inverse(grads, cosine_table, sine_table):
    half = grads.shape[-1] // 2
    shifted = grads * sine_table
    turned = jnp.concatenate([shifted[..., half:], -shifted[..., :half]], -1)
    return grads * cosine_table + turned


def block_scores(query_block, key_block, segment, first, limit):
    scores = jnp.einsum(
        "qkgd,tkd->kgqt", query_block, key_block, preferred_element_type=jnp.float32
    ) * HEAD_SIZE ** (-0.5)
    rows = jnp.arange(first, limit, dtype=jnp.int32)
    columns = jnp.arange(limit, dtype=jnp.int32)
    allowed = (segment[first:limit][:, None] == segment[:limit][None, :]) & (
        columns[None, :] <= rows[:, None]
    )
    return jnp.where(allowed, scores, -1e30)


def forward_layer(hidden_in, weights, lengths):
    gain_one, w_q, w_kv, w_o, gain_two, w_gu, w_d = weights
    token_count = hidden_in.shape[0]
    query_group_size = QUERY_HEADS // KEY_VALUE_HEADS
    segment, place = positions(lengths, token_count)
    cosine_table, sine_table = rope_tables(place, HEAD_SIZE)
    scale_in = lax.rsqrt(jnp.mean(hidden_in * hidden_in, -1, keepdims=True) + EPS)
    normed = (hidden_in * scale_in * gain_one).astype(jnp.bfloat16)
    query_single = jnp.dot(normed, w_q, preferred_element_type=jnp.float32)
    key_value_rows = jnp.dot(normed, w_kv, preferred_element_type=jnp.float32)
    query_rows = (
        rotary_apply(
            query_single.reshape(token_count, QUERY_HEADS, HEAD_SIZE), cosine_table, sine_table
        )
        .astype(jnp.bfloat16)
        .reshape(token_count, KEY_VALUE_HEADS, query_group_size, HEAD_SIZE)
    )
    key_rows = rotary_apply(
        key_value_rows[:, : KEY_VALUE_HEADS * HEAD_SIZE].reshape(
            token_count, KEY_VALUE_HEADS, HEAD_SIZE
        ),
        cosine_table,
        sine_table,
    ).astype(jnp.bfloat16)
    value_rows = (
        key_value_rows[:, KEY_VALUE_HEADS * HEAD_SIZE :]
        .reshape(token_count, KEY_VALUE_HEADS, HEAD_SIZE)
        .astype(jnp.bfloat16)
    )
    block = token_count // 2
    pieces = []
    totals = []
    for part in range(2):
        first = part * block
        limit = first + block
        scores = block_scores(query_rows[first:limit], key_rows[:limit], segment, first, limit)
        peak = jnp.max(scores, -1, keepdims=True)
        expo = jnp.exp(scores - peak)
        summed = jnp.sum(expo, -1, keepdims=True)
        prob = (expo / summed).astype(jnp.bfloat16)
        totals.append(peak + jnp.log(summed))
        attended_block = jnp.einsum(
            "kgqt,tkd->qkgd", prob, value_rows[:limit], preferred_element_type=jnp.float32
        )
        pieces.append(attended_block.reshape(block, QUERY_HEADS * HEAD_SIZE))
    attended = jnp.concatenate(pieces, 0).astype(jnp.bfloat16)
    mixed = hidden_in + jnp.dot(attended, w_o, preferred_element_type=jnp.float32)
    scale_mid = lax.rsqrt(jnp.mean(mixed * mixed, -1, keepdims=True) + EPS)
    normed_two = (mixed * scale_mid * gain_two).astype(jnp.bfloat16)
    gateup = jnp.dot(normed_two, w_gu, preferred_element_type=jnp.float32)
    inner = (jax.nn.silu(gateup[:, :FF]) * gateup[:, FF:]).astype(jnp.bfloat16)
    result = mixed + jnp.dot(inner, w_d, preferred_element_type=jnp.float32)
    kept = (
        hidden_in,
        scale_in,
        normed,
        query_rows,
        key_rows,
        value_rows,
        totals,
        attended,
        mixed,
        scale_mid,
        normed_two,
        gateup,
        inner,
        segment,
        cosine_table,
        sine_table,
    )
    return (result, kept)


def backward_layer(grad_result, weights, kept):
    gain_one, w_q, w_kv, w_o, gain_two, w_gu, w_d = weights
    (
        hidden_in,
        scale_in,
        normed,
        query_rows,
        key_rows,
        value_rows,
        totals,
        attended,
        mixed,
        scale_mid,
        normed_two,
        gateup,
        inner,
        segment,
        cosine_table,
        sine_table,
    ) = kept
    token_count = hidden_in.shape[0]
    query_group_size = QUERY_HEADS // KEY_VALUE_HEADS
    grad_low = grad_result.astype(jnp.bfloat16)
    grad_wd = jnp.einsum("tf,td->fd", inner, grad_low, preferred_element_type=jnp.float32)
    grad_inner = jnp.einsum("td,fd->tf", grad_low, w_d, preferred_element_type=jnp.float32)
    gate = gateup[:, :FF]
    upper = gateup[:, FF:]
    sigma = jax.nn.sigmoid(gate)
    slope = sigma * (1.0 + gate * (1.0 - sigma))
    grad_gateup = jnp.concatenate(
        [grad_inner * upper * slope, grad_inner * gate * sigma], 1
    ).astype(jnp.bfloat16)
    grad_wgu = jnp.einsum("td,tf->df", normed_two, grad_gateup, preferred_element_type=jnp.float32)
    grad_normed_two = jnp.einsum("tf,df->td", grad_gateup, w_gu, preferred_element_type=jnp.float32)
    grad_gain_two = jnp.sum(grad_normed_two * mixed * scale_mid, 0)
    weighted_two = grad_normed_two * gain_two
    grad_mixed = (
        grad_result
        + scale_mid * weighted_two
        - mixed * scale_mid**3 * jnp.mean(weighted_two * mixed, -1, keepdims=True)
    )
    grad_branch = grad_mixed.astype(jnp.bfloat16)
    grad_wo = jnp.einsum("tc,td->cd", attended, grad_branch, preferred_element_type=jnp.float32)
    attended_gradient = jnp.einsum(
        "td,cd->tc", grad_branch, w_o, preferred_element_type=jnp.float32
    ).astype(jnp.bfloat16)
    attended_gradient = attended_gradient.reshape(
        token_count, KEY_VALUE_HEADS, query_group_size, HEAD_SIZE
    )
    block = token_count // 2
    grad_queries = []
    key_gradient = jnp.zeros((token_count, KEY_VALUE_HEADS, HEAD_SIZE), jnp.float32)
    value_gradient = jnp.zeros((token_count, KEY_VALUE_HEADS, HEAD_SIZE), jnp.float32)
    for part in range(2):
        first = part * block
        limit = first + block
        scores = block_scores(query_rows[first:limit], key_rows[:limit], segment, first, limit)
        prob = jnp.exp(scores - totals[part])
        grad_block = attended_gradient[first:limit]
        grad_prob = jnp.einsum(
            "qkgd,tkd->kgqt", grad_block, value_rows[:limit], preferred_element_type=jnp.float32
        )
        delta = jnp.sum(prob * grad_prob, -1, keepdims=True)
        grad_scores = (prob * (grad_prob - delta)).astype(jnp.bfloat16)
        grad_queries.append(
            jnp.einsum(
                "kgqt,tkd->qkgd", grad_scores, key_rows[:limit], preferred_element_type=jnp.float32
            )
            * HEAD_SIZE ** (-0.5)
        )
        key_gradient = key_gradient.at[:limit].add(
            jnp.einsum(
                "kgqt,qkgd->tkd",
                grad_scores,
                query_rows[first:limit],
                preferred_element_type=jnp.float32,
            )
            * HEAD_SIZE ** (-0.5)
        )
        value_gradient = value_gradient.at[:limit].add(
            jnp.einsum(
                "kgqt,qkgd->tkd",
                prob.astype(jnp.bfloat16),
                grad_block,
                preferred_element_type=jnp.float32,
            )
        )
    grad_query = rotary_inverse(
        jnp.concatenate(grad_queries, 0).reshape(token_count, QUERY_HEADS, HEAD_SIZE),
        cosine_table,
        sine_table,
    )
    grad_query = grad_query.reshape(token_count, QUERY_HEADS * HEAD_SIZE).astype(jnp.bfloat16)
    grad_keyval = jnp.concatenate(
        [
            rotary_inverse(key_gradient, cosine_table, sine_table).reshape(
                token_count, KEY_VALUE_HEADS * HEAD_SIZE
            ),
            value_gradient.reshape(token_count, KEY_VALUE_HEADS * HEAD_SIZE),
        ],
        1,
    ).astype(jnp.bfloat16)
    grad_wq = jnp.einsum("td,tc->dc", normed, grad_query, preferred_element_type=jnp.float32)
    grad_wkv = jnp.einsum("td,tc->dc", normed, grad_keyval, preferred_element_type=jnp.float32)
    grad_normed = jnp.einsum("tc,dc->td", grad_query, w_q, preferred_element_type=jnp.float32)
    grad_normed = grad_normed + jnp.einsum(
        "tc,dc->td", grad_keyval, w_kv, preferred_element_type=jnp.float32
    )
    grad_gain_one = jnp.sum(grad_normed * hidden_in * scale_in, 0)
    weighted_one = grad_normed * gain_one
    grad_input = (
        grad_mixed
        + scale_in * weighted_one
        - hidden_in * scale_in**3 * jnp.mean(weighted_one * hidden_in, -1, keepdims=True)
    )
    return (
        grad_input,
        (grad_gain_one, grad_wq, grad_wkv, grad_wo, grad_gain_two, grad_wgu, grad_wd),
    )


def shards(
    inputs,
    cotangent,
    seq_lengths,
    attn_gain,
    w_query,
    key_value_weight,
    w_out,
    ffn_gain,
    w_gateup,
    w_down,
):
    gathered = (
        lax.all_gather(attn_gain, "fsdp", axis=1, tiled=True),
        lax.all_gather(w_query, "fsdp", axis=1, tiled=True),
        lax.all_gather(key_value_weight, "fsdp", axis=1, tiled=True),
        lax.all_gather(w_out, "fsdp", axis=1, tiled=True),
        lax.all_gather(ffn_gain, "fsdp", axis=1, tiled=True),
        lax.all_gather(w_gateup, "fsdp", axis=1, tiled=True),
        lax.all_gather(w_down, "fsdp", axis=1, tiled=True),
    )
    weights = tuple((w[0] for w in gathered))
    section = lax.axis_index("section")
    at_first = section == 0
    width = inputs.shape[1]
    x_slots = inputs.reshape(MICRO, -1, width)
    cot_slots = cotangent.reshape(MICRO, -1, width)
    sums = tuple((jnp.zeros(w.shape, jnp.float32) for w in weights))
    forward_outs = []
    backward_outs = []
    received = jnp.zeros_like(x_slots[0])
    grad_received = jnp.zeros_like(x_slots[0])
    recent = {}
    for tick in range(MICRO + 2):
        if tick <= MICRO:
            current = jnp.where(at_first, x_slots[min(tick, MICRO - 1)], received)
            slot = jnp.clip(tick - section, 0, MICRO - 1)
            lengths = lax.dynamic_index_in_dim(seq_lengths, slot, 0, keepdims=False)
            result, kept_now = forward_layer(current.astype(jnp.float32), weights, lengths)
            outgoing = result.astype(jnp.bfloat16)
            forward_outs.append(outgoing)
            recent[tick] = kept_now
            if tick < MICRO:
                received = shifted_2(outgoing, "section", 1)
        if tick >= 1:
            incoming = jnp.where(
                at_first, grad_received, cot_slots[min(tick - 1, MICRO - 1)]
            ).astype(jnp.float32)
            kept = jax.tree.map(
                lambda early, late: jnp.where(at_first, early, late),
                recent[max(tick - 2, 0)],
                recent[min(tick, MICRO)],
            )
            slot_index = tick - 2 + section
            valid = ((slot_index >= 0) & (slot_index < MICRO)).astype(jnp.float32)
            grad_input, grads = backward_layer(incoming, weights, kept)
            sums = tuple((total + valid * grad for total, grad in zip(sums, grads)))
            backward_outs.append(grad_input)
            if tick <= MICRO:
                grad_received = shifted_2(grad_input.astype(jnp.bfloat16), "section", -1)
            if tick >= 2:
                recent.pop(tick - 2, None)
    acts = jnp.concatenate(
        [jnp.where(at_first, forward_outs[m], forward_outs[m + 1]) for m in range(MICRO)], 0
    )
    in_grads = jnp.concatenate(
        [jnp.where(at_first, backward_outs[m + 1], backward_outs[m]) for m in range(MICRO)], 0
    )
    sum_gain_one, sum_query, sum_keyval, sum_out, sum_gain_two, sum_gateup, sum_down = [
        s[None] for s in sums
    ]
    summed = (
        lax.psum(sum_gain_one.astype(jnp.bfloat16), "replica").astype(jnp.float32),
        lax.psum(sum_query.astype(jnp.bfloat16), "replica").astype(jnp.float32),
        lax.psum(sum_keyval.astype(jnp.bfloat16), "replica").astype(jnp.float32),
        lax.psum(sum_out.astype(jnp.bfloat16), "replica").astype(jnp.float32),
        lax.psum(sum_gain_two.astype(jnp.bfloat16), "replica").astype(jnp.float32),
        lax.psum(sum_gateup.astype(jnp.bfloat16), "replica").astype(jnp.float32),
        lax.psum(sum_down.astype(jnp.bfloat16), "replica").astype(jnp.float32),
    )
    shares = (
        lax.psum_scatter(
            summed[0].astype(jnp.bfloat16), "fsdp", scatter_dimension=1, tiled=True
        ).astype(jnp.float32),
        lax.psum_scatter(
            summed[1].astype(jnp.bfloat16), "fsdp", scatter_dimension=1, tiled=True
        ).astype(jnp.float32),
        lax.psum_scatter(
            summed[2].astype(jnp.bfloat16), "fsdp", scatter_dimension=1, tiled=True
        ).astype(jnp.float32),
        lax.psum_scatter(
            summed[3].astype(jnp.bfloat16), "fsdp", scatter_dimension=1, tiled=True
        ).astype(jnp.float32),
        lax.psum_scatter(
            summed[4].astype(jnp.bfloat16), "fsdp", scatter_dimension=1, tiled=True
        ).astype(jnp.float32),
        lax.psum_scatter(
            summed[5].astype(jnp.bfloat16), "fsdp", scatter_dimension=1, tiled=True
        ).astype(jnp.float32),
        lax.psum_scatter(
            summed[6].astype(jnp.bfloat16), "fsdp", scatter_dimension=1, tiled=True
        ).astype(jnp.float32),
    )
    return (
        acts[None],
        in_grads[None],
        shares[0],
        shares[1],
        shares[2],
        shares[3],
        shares[4],
        shares[5],
        shares[6],
    )


def solution(mesh):
    return jax.shard_map(
        shards,
        mesh=mesh,
        in_specs=(
            P(("fsdp", "replica"), None),
            P(("fsdp", "replica"), None),
            P(("fsdp", "replica"), None),
            P("section", "fsdp"),
            P("section", "fsdp", None),
            P("section", "fsdp", None),
            P("section", "fsdp", None),
            P("section", "fsdp"),
            P("section", "fsdp", None),
            P("section", "fsdp", None),
        ),
        out_specs=(
            P("section", ("fsdp", "replica"), None),
            P("section", ("fsdp", "replica"), None),
            P("section", "fsdp"),
            P("section", "fsdp", None),
            P("section", "fsdp", None),
            P("section", "fsdp", None),
            P("section", "fsdp"),
            P("section", "fsdp", None),
            P("section", "fsdp", None),
        ),
        check_vma=False,
    )
```

profile of v0, /device:TPU:0, one launch (start us, length us, event | category | flops | bytes accessed | tf_op | source)
XLA Modules:
  0.0 690.6 jit_solution(15135257465707068189)
XLA Ops:
  9.3 11.6 %all_gather.22 = bf16[1,576,384]{2,1,0:T(8,128)(2,1)S(1)} all-gather(bf16[1,144,384]{2,1,0:T(8,128)(2,1)} %param.51), channel_id=1, replica_groups=mesh['section'=2,'fsdp'=4,'replica'=4] {'fsdp'}, dimensions={1}, use_global_device_ids=true | all-gather | bytes 552960 | tf_op jit(solution)/shard_map/all_gather | solution.py:274
  24.7 9.0 %all-reduce.16 = (bf16[576]{0:T(1024)(128)(2,1)S(1)}, bf16[576]{0:T(1024)(128)(2,1)S(1)}) all-reduce(bf16[576]{0:T(1024)(128)(2,1)S(1)} %dynamic-update-slice.30, bf16[576]{0:T(1024)(128)(2,1)S(1)} %dynamic-update-slice.31), channel_id=1, replica_groups=mesh['section'=2,'fsdp'=4,'replica'=4] {'fsdp'}, use_global_device_ids=true, to_apply=%add.6 | all-reduce | flops 1152 | bytes 4608
  47.7 17.7 %all_gather.24 = bf16[1,576,576]{2,1,0:T(8,128)(2,1)S(1)} all-gather(bf16[1,144,576]{2,1,0:T(8,128)(2,1)S(1)} %copy-done.160), channel_id=1, replica_groups=mesh['section'=2,'fsdp'=4,'replica'=4] {'fsdp'}, dimensions={1}, use_global_device_ids=true | all-gather | bytes 829440 | tf_op jit(solution)/shard_map/all_gather | solution.py:275
  67.2 10.4 %all_gather.23 = bf16[1,576,576]{2,1,0:T(8,128)(2,1)S(1)} all-gather(bf16[1,144,576]{2,1,0:T(8,128)(2,1)S(1)} %copy-done.161), channel_id=1, replica_groups=mesh['section'=2,'fsdp'=4,'replica'=4] {'fsdp'}, dimensions={1}, use_global_device_ids=true | all-gather | bytes 829440 | tf_op jit(solution)/shard_map/all_gather | solution.py:273
  101.4 6.4 fusion.77
  190.1 25.2 %broadcast_select_fusion = (f32[768,3072]{1,0:T(8,128)}, f32[768,3072]{1,0:T(8,128)}, f32[768,3072]{1,0:T(8,128)}, f32[768,3072]{1,0:T(8,128)}) fusion(f32[768,3072]{1,0:T(8,128)} %copy-done.2, pred[]{:T(512)S(6)} %eq.74, f32[768,3072]{1,0:T(8,128)} %copy-done.1, bf16[768,576]{0,1:T(8,128)(2,1)} %multiply_convert_fusion.3, ...), kind=kOutput, calls=%fused_computation.109 | convolution fusion | flops 2724986880 | bytes 61046784 | tf_op jit(solution)/shard_map/dot_general | solution.py:114
  215.4 8.7 %fusion.56 = (bf16[768,1536]{1,0:T(8,128)(2,1)S(1)}, bf16[768,1536]{1,0:T(8,128)(2,1)S(1)}) fusion(f32[768,3072]{1,0:T(8,128)} %get-tuple-element.269, bf16[1,1536,576]{1,2,0:T(8,128)(2,1)} %all-gather.5.cloned.1.call-done, bf16[1536,576]{0,1:T(8,128)(2,1)} %param.47, pred[]{:T(512)S(6)} %eq.74), kind=kOutput, calls=%fused_computation.93 | convolution fusion | flops 1374732288 | bytes 16809984 | tf_op jit(solution)/shard_map/td,fd->tf/dot_general | solution.py:162
  288.3 7.5 %fusion.54 = (bf16[768,1536]{1,0:T(8,128)(2,1)}, bf16[768,1536]{1,0:T(8,128)(2,1)}) fusion(f32[768,3072]{1,0:T(8,128)} %get-tuple-element.268, bf16[768,576]{0,1:T(8,128)(2,1)S(1)} %broadcast_select_fusion.13, bf16[1,1536,576]{1,2,0:T(8,128)(2,1)S(1)} %copy-done.231), kind=kOutput, calls=%fused_computation.90 | convolution fusion | flops 1374289920 | bytes 16809984 | tf_op jit(solution)/shard_map/td,fd->tf/dot_general | solution.py:162
  295.8 8.9 %multiply_reduce_fusion.1 = (f32[576]{0:T(1024)}, f32[768]{0:T(1024)S(1)}, f32[768,576]{0,1:T(8,128)S(1)}, f32[768,576]{0,1:T(8,128)}) fusion(f32[768]{0:T(1024)S(1)} %copy-done.218, f32[576]{0:T(1024)S(1)} %mul.1346, f32[768,576]{0,1:T(8,128)} %copy-done.117, f32[768,576]{0,1:T(8,128)S(1)} %copy-done.112, pred[]{:T(512)S(6)} %eq.74, ...), kind=kOutput, calls=%fused_computation.228 | convolution fusion | flops 2730441472 | bytes 15346177 | tf_op jit(solution)/shard_map/tf,df->td/dot_general | solution.py:171
  324.0 6.0 fusion.5
  330.0 6.2 fusion.7
  371.5 6.8 multiply_reduce_fusion
  380.9 5.8 fusion
  386.7 6.6 fusion.2
  403.0 6.0 fusion.81
  409.0 8.7 %copy.164 = bf16[1,1536,576]{2,0,1:T(2,128)(2,1)} copy(bf16[1,1536,576]{1,2,0:T(8,128)(2,1)} %fusion.81) | data formatting | bytes 3538944
  452.1 7.7 %fusion.80 = f32[576,3072]{1,0:T(8,128)} fusion(bf16[768,1536]{1,0:T(8,128)(2,1)} %copy-done.252, bf16[768,1536]{1,0:T(8,128)(2,1)S(1)} %copy-done.251, bf16[768,576]{0,1:T(8,128)(2,1)S(1)} %copy-done.89, bf16[768,576]{0,1:T(8,128)(2,1)S(1)} %copy-done.91, pred[]{:T(512)S(6)} %eq.74), kind=kOutput, calls=%fused_computation.146 | convolution fusion | flops 2727788544 | bytes 13565953 | tf_op jit(solution)/shard_map/td,tf->df/dot_general | solution.py:170
  469.1 7.3 %fusion.63 = bf16[1,576,3072]{2,1,0:T(8,128)(2,1)} fusion(f32[576,3072]{1,0:T(8,128)S(1)} %fusion.79, f32[576,3072]{1,0:T(8,128)} %fusion.80, f32[]{:T(128)S(6)} %convert_element_type.433, f32[]{:T(128)S(6)} %convert_element_type.432, f32[]{:T(128)S(6)} %convert_element_type.431, bf16[768,1536]{1,0:T(8,128)(2,1)S(1)} %copy-done.247, ...), kind=kOutput, calls=%fused_computation.115 | convolution fusion | flops 2738405376 | bytes 24182796 | tf_op jit(solution)/shard_map/td,tf->df/dot_general | solution.py:170
  489.5 22.8 %reduce-scatter.25.cloned.1.call-done = bf16[1,144,576]{2,1,0:T(8,128)(2,1)} async-done(((bf16[1,576,576]{2,1,0:T(8,128)(2,1)}), bf16[1,144,576]{2,1,0:T(8,128)(2,1)}) %reduce-scatter.25.cloned.1.call-update) | async-done | bytes 165904
  512.3 28.9 %reduce-scatter.29.cloned.1.call-done = bf16[1,144,576]{2,1,0:T(8,128)(2,1)} async-done(((bf16[1,576,576]{2,1,0:T(8,128)(2,1)}), bf16[1,144,576]{2,1,0:T(8,128)(2,1)}) %reduce-scatter.29.cloned.1.call-update) | async-done | bytes 165904
  541.2 51.2 %reduce-scatter.21.cloned.1.call-done = bf16[1,144,3072]{2,1,0:T(8,128)(2,1)} async-done(((bf16[1,576,3072]{2,1,0:T(8,128)(2,1)}), bf16[1,144,3072]{2,1,0:T(8,128)(2,1)}) %reduce-scatter.21.cloned.1.call-update) | async-done | bytes 884752 | tf_op jit(solution)/shard_map/reduce_scatter | solution.py:355
  598.2 9.7 %all-reduce.15 = (bf16[1,576]{1,0:T(2,128)(2,1)}, bf16[1,576]{1,0:T(2,128)(2,1)}) all-reduce(bf16[1,576]{1,0:T(2,128)(2,1)S(1)} %convert_element_type.435, bf16[1,576]{1,0:T(2,128)(2,1)} %convert_element_type.450), channel_id=2, replica_groups=mesh['section'=2,'fsdp'=4,'replica'=4] {'fsdp'}, use_global_device_ids=true, to_apply=%region_43.44.clone | all-reduce | flops 1152 | bytes 4608
  610.0 13.2 %all-reduce.13 = (bf16[1,144]{1,0:T(2,128)(2,1)}, bf16[1,144]{1,0:T(2,128)(2,1)}) all-reduce(bf16[1,144]{1,0:T(2,128)(2,1)S(1)} %constant_dynamic-slice_fusion.1, bf16[1,144]{1,0:T(2,128)(2,1)} %constant_dynamic-slice_fusion), channel_id=1, replica_groups=mesh['section'=2,'fsdp'=4,'replica'=4] {'replica'}, use_global_device_ids=true, to_apply=%region_42.43 | all-reduce | flops 288 | bytes 1152 | tf_op jit(solution)/shard_map/psum | solution.py:331
  631.4 43.6 %all-reduce.19.cloned.1.call-done = (bf16[1,144,576]{2,1,0:T(8,128)(2,1)}, bf16[1,144,384]{2,1,0:T(8,128)(2,1)}, bf16[1,144,576]{2,1,0:T(8,128)(2,1)}, bf16[1,144,3072]{2,1,0:T(8,128)(2,1)}, bf16[1,384,576]{1,2,0:T(8,128)(2,1)}) async-done(((bf16[1,144,576]{2,1,0:T(8,128)(2,1)}, bf16[1,144,384]{2,1,0:T(8,128)(2,1)}, bf16[1,144,576]{2,1,0:T(8,128)(2,1)}, bf16[1,144,3072]{2,1,0:T(8,128)(2,1)}, ...) | async-done | bytes 1769488 | tf_op jit(solution)/shard_map/psum | solution.py:332
  (805 shorter events, 335.5 us)
Async XLA Ops:
  7.2 94.2 %all-gather.3.cloned.1.call-start = ((), (), s32[]{:S(2)}) async-start(), calls=%async_computation.5 | async-start | bytes 4423680 | tf_op jit(solution)/shard_map/all_gather | solution.py:277
  7.9 106.0 %all-gather.5.cloned.1.call-start = ((), (), s32[]{:S(2)}) async-start(), calls=%async_computation.6 | async-start | bytes 2211840 | tf_op jit(solution)/shard_map/all_gather | solution.py:278
  8.7 477.5 %reduce-scatter.23.cloned.1.call-start = ((), (), s32[]{:S(2)}) async-start(), calls=%async_computation.8 | async-start | bytes 2457600
  33.7 44.3 %copy-start.172 = (f32[576]{0:T(1024)}, f32[576]{0:T(1024)S(1)}, u32[]{:S(2)}) copy-start(f32[576]{0:T(1024)S(1)} %mul.1345) | copy-start | bytes 6916
  37.9 40.1 %copy-start.221 = (f32[768]{0:T(1024)}, f32[768]{0:T(1024)S(1)}, u32[]{:S(2)}) copy-start(f32[768]{0:T(1024)S(1)} %add_rsqrt_fusion.5) | copy-start | bytes 9220
  65.4 163.0 %copy-start.33 = (bf16[1,576,576]{2,1,0:T(8,128)(2,1)}, bf16[1,576,576]{2,1,0:T(8,128)(2,1)S(1)}, u32[]{:S(2)}) copy-start(bf16[1,576,576]{2,1,0:T(8,128)(2,1)S(1)} %all_gather.24) | copy-start | bytes 1990660
  80.9 45.9 %copy-start.31 = (bf16[768,9,64]{0,2,1:T(8,128)(2,1)}, bf16[768,9,64]{0,2,1:T(8,128)(2,1)S(1)}, u32[]{:S(2)}) copy-start(bf16[768,9,64]{0,2,1:T(8,128)(2,1)S(1)} %fusion.115) | copy-start | bytes 2654212
  118.4 4.6 collective-permute-start
  123.4 157.8 %copy-start.24 = (bf16[768,576]{0,1:T(8,128)(2,1)}, bf16[768,576]{0,1:T(8,128)(2,1)S(1)}, u32[]{:S(2)}) copy-start(bf16[768,576]{0,1:T(8,128)(2,1)S(1)} %get-tuple-element.260) | copy-start | bytes 2654212
  153.0 13.9 %collective-permute-start.1 = (bf16[768,576]{0,1:T(8,128)(2,1)S(1)}, bf16[768,576]{0,1:T(8,128)(2,1)S(1)}, u32[]{:S(2)}, u32[]{:S(2)}) collective-permute-start(bf16[768,576]{0,1:T(8,128)(2,1)S(1)} %get-tuple-element.406), channel_id=1, source_target_pairs={{0,16},{1,17},{2,18},{3,19},{4,20},{5,21},{6,22},{7,23},{8,24},{9,... | collective-permute-start | bytes 2654216 | tf_op jit(solution)/shard_map/ppermute | solution.py:20
  174.3 97.4 %copy-start.52 = (bf16[768,3,64]{0,2,1:T(8,128)(2,1)}, bf16[768,3,64]{0,2,1:T(8,128)(2,1)S(1)}, u32[]{:S(2)}) copy-start(bf16[768,3,64]{0,2,1:T(8,128)(2,1)S(1)} %get-tuple-element.432) | copy-start | bytes 884740
  179.0 65.7 %copy-start.166 = (f32[3,3,384]{2,1,0:T(4,128)}, f32[3,3,384]{2,1,0:T(4,128)S(1)}, u32[]{:S(2)}) copy-start(f32[3,3,384]{2,1,0:T(4,128)S(1)} %get-tuple-element.337) | copy-start | bytes 41476
  185.1 47.3 %copy-start.171 = (f32[3,3,384]{2,1,0:T(4,128)}, f32[3,3,384]{2,1,0:T(4,128)S(1)}, u32[]{:S(2)}) copy-start(f32[3,3,384]{2,1,0:T(4,128)S(1)} %get-tuple-element.335) | copy-start | bytes 41476
  190.1 40.1 %slice-start.10 = ((s8[5308416]{0:T(1024)(128)(4,1)}), s8[1114112]{0:T(1024)(128)(4,1)S(1)}, s32[]{:S(2)}) async-start(s8[5308416]{0:T(1024)(128)(4,1)} %bitcast.838), calls=%async_computation.23 | async-start | bytes 2228224
  265.2 21.3 %collective-permute-start.2 = (bf16[768,576]{0,1:T(8,128)(2,1)}, bf16[768,576]{0,1:T(8,128)(2,1)S(1)}, u32[]{:S(2)}, u32[]{:S(2)}) collective-permute-start(bf16[768,576]{0,1:T(8,128)(2,1)} %get-tuple-element.246), channel_id=1, source_target_pairs={{16,0},{17,1},{18,2},{19,3},{20,4},{21,5},{22,6},{23,7},{24,8},{25... | collective-permute-start | bytes 2654216 | tf_op jit(solution)/shard_map/ppermute | solution.py:20
  270.0 40.6 %copy-start.4 = (f32[3,384,384,3]{2,1,3,0:T(8,128)}, f32[3,384,384,3]{2,1,3,0:T(8,128)S(1)}, u32[]{:S(2)}) copy-start(f32[3,384,384,3]{2,1,3,0:T(8,128)S(1)} %fusion.325) | copy-start | bytes 15925252
  271.6 115.1 %copy-start = (f32[3,768,384,3]{2,1,3,0:T(8,128)}, f32[3,768,384,3]{2,1,3,0:T(8,128)S(1)}, u32[]{:S(2)}) copy-start(f32[3,768,384,3]{2,1,3,0:T(8,128)S(1)} %fusion.304) | copy-start | bytes 31850500
  354.6 9.7 %collective-permute-start.3 = (bf16[768,576]{0,1:T(8,128)(2,1)S(1)}, bf16[768,576]{0,1:T(8,128)(2,1)S(1)}, u32[]{:S(2)}, u32[]{:S(2)}) collective-permute-start(bf16[768,576]{0,1:T(8,128)(2,1)S(1)} %convert_element_type.421), channel_id=1, source_target_pairs={{16,0},{17,1},{18,2},{19,3},{20,4},{21,5},{22,6},{23,7},{24,8},{25... | collective-permute-start | bytes 2654216 | tf_op jit(solution)/shard_map/ppermute | solution.py:20
  421.6 67.9 %reduce-scatter.27.cloned.1.call-start = ((), (), s32[]{:S(2)}) async-start(), calls=%async_computation.10 | async-start | bytes 552960
  442.2 70.1 %reduce-scatter.25.cloned.1.call-start = ((), (), s32[]{:S(2)}) async-start(), calls=%async_computation.9 | async-start | bytes 921600
  449.3 91.8 %reduce-scatter.29.cloned.1.call-start = ((), (), s32[]{:S(2)}) async-start(), calls=%async_computation.11 | async-start | bytes 921600
  463.4 128.9 %reduce-scatter.21.cloned.1.call-start = ((), (), s32[]{:S(2)}) async-start(), calls=%async_computation.7 | async-start | bytes 4423680 | tf_op jit(solution)/shard_map/reduce_scatter | solution.py:355
  476.4 198.6 %all-reduce.19.cloned.1.call-start = ((), (), s32[]{:S(2)}) async-start(), calls=%async_computation.12 | async-start | bytes 3612672 | tf_op jit(solution)/shard_map/psum | solution.py:332
  486.2 106.2 %copy-start.207 = (f32[768]{0:T(1024)S(1)}, f32[768]{0:T(1024)}, u32[]{:S(2)}) copy-start(f32[768]{0:T(1024)} %get-tuple-element.233) | copy-start | bytes 9220
  (259 other events, 1197.8 us)
Sparse Core Ops, SparseCore 0:
  9.9 55.9 all-gather.2
  67.7 32.4 all-gather.4
  421.7 34.7 reduce-scatter.22
  459.2 24.2 reduce-scatter.26
  486.5 25.7 reduce-scatter.24
  515.4 25.7 reduce-scatter.28
  545.1 47.2 reduce-scatter.20
  595.9 79.0 all-reduce.18
where the time goes:
time: 699 us; the launch traced here: 691 us
  matrix products  266 us (38%)
  waiting for transfers between devices  148 us (21%)
  other arithmetic  111 us (16%)
  blocking collectives  71.6 us (10%)
  local copies, waits for them, and re-layouts  68.9 us (10%)
  between operations  19.1 us (3%)
    unnamed x553, local copies, waits for them, and re-layouts  56.2 us
    unnamed x12, waiting for transfers between devices  53.2 us
    reduce_scatter x1, waiting for transfers between devices, shards(): lax.psum_scatter(summed[5].astype(jnp.bfloat16), 'fsdp', scatter_dimensio...  51.2 us
    psum x1, waiting for transfers between devices, shards(): lax.psum(sum_query.astype(jnp.bfloat16), 'replica').astype(jnp.float32)  43.6 us
    dot_general x3, matrix products, forward_layer(): gateup = jnp.dot(normed_two, w_gu, preferred_element_type=jnp.float32)  35.6 us
    dot_general x12, matrix products, block_scores(): jnp.einsum('qkgd,tkd->kgqt', query_block, key_block, preferred_element_ty...  26.8 us
    convert_element_type x6, other arithmetic, backward_layer(): grad_scores = (prob * (grad_prob - delta)).astype(jnp.bfloat16)  25.2 us
    dot_general x6, matrix products, backward_layer(): jnp.einsum('qkgd,tkd->kgqt', grad_block, value_rows[:limit], preferred_el...  23.6 us
  transfers between devices with their start and end apart: 12, of which 4 were waited for; matrix products, arithmetic and copies ran while one was open for 24% of the time, Pallas kernels for 0%

commit v1 on v0

v1 whole, which is shorter than its diff:
```python
import functools

import jax
import jax.numpy as jnp
from jax import lax
from jax.experimental import pallas as pl
from jax.experimental.pallas import tpu as pltpu
from jax.sharding import PartitionSpec as P

QUERY_HEADS = 9
KEY_VALUE_HEADS = 3
GROUP = 3
HEAD_SIZE = 64
FF = 1536
MICRO = 2
EPS = 1e-05
ROPE_BASE = 100000.0
Q_BLOCK = 256
LIMIT = 56 * 1024 * 1024
BF = jnp.bfloat16
F32 = jnp.float32


def positions(lengths, token_count):
    ends = jnp.cumsum(lengths)
    index = jnp.arange(token_count, dtype=jnp.int32)
    after = index[:, None] >= ends[None, :]
    start = jnp.sum(jnp.where(after, lengths[None, :], 0), 1)
    return start, index - start


def rope_tables(place):
    half = HEAD_SIZE // 2
    freq = ROPE_BASE ** (-(jnp.arange(half, dtype=F32) * 2.0 / HEAD_SIZE))
    angle = place.astype(F32)[:, None] * freq[None, :]
    cosine, sine = jnp.cos(angle), jnp.sin(angle)
    return (
        jnp.concatenate([cosine] * 4, 1),
        jnp.concatenate([-sine, sine, -sine, sine], 1),
    )


def turned(x):
    lane = lax.broadcasted_iota(jnp.int32, x.shape, 1)
    first = (lane % HEAD_SIZE) < HEAD_SIZE // 2
    return jnp.where(first, pltpu.roll(x, 96, 1), pltpu.roll(x, 32, 1))


def fill_bias(bias, start_ref):
    tokens = bias.shape[0]
    start = start_ref[...]
    for first in range(0, tokens, 128):
        key = lax.broadcasted_iota(jnp.int32, (128, tokens), 0) + first
        query = lax.broadcasted_iota(jnp.int32, (128, tokens), 1)
        ok = (key >= start) & (key <= query)
        bias[first : first + 128, :] = jnp.where(ok, 0.0, -1e30)


def dot_t(a, b):
    return lax.dot_general(a, b, (((1,), (1,)), ((), ())), preferred_element_type=F32)


def dot_0(a, b):
    return lax.dot_general(a, b, (((0,), (0,)), ((), ())), preferred_element_type=F32)


def attention_forward(qkv_ref, cos_ref, sin_ref, start_ref, att_ref, q_ref, k_ref, v_ref, lse_ref, bias, o_s):
    tokens = qkv_ref.shape[0]
    fill_bias(bias, start_ref)
    cosine, sine = cos_ref[...], sin_ref[...]
    for chunk in range(6):
        x = qkv_ref[:, chunk * 128 : chunk * 128 + 128]
        x = x * cosine + turned(x) * sine
        for side in range(2):
            head = chunk * 2 + side
            part = x[:, side * 64 : side * 64 + 64]
            if head < QUERY_HEADS:
                q_ref[head] = (part * HEAD_SIZE ** (-0.5)).astype(BF)
            else:
                k_ref[head - QUERY_HEADS] = part.astype(BF)
    for head in range(KEY_VALUE_HEADS):
        v_ref[head] = qkv_ref[:, 768 + head * 64 : 832 + head * 64].astype(BF)

    def group(g, _):
        for first in range(0, tokens, Q_BLOCK):
            limit = first + Q_BLOCK
            queries = q_ref[pl.ds(g * GROUP, GROUP), first:limit, :].reshape(GROUP * Q_BLOCK, HEAD_SIZE)
            scores = dot_t(k_ref[g, :limit, :], queries)
            mask = bias[:limit, first:limit]
            probs = []
            for head in range(GROUP):
                s = scores[:, head * Q_BLOCK : (head + 1) * Q_BLOCK] + mask
                peak = jnp.max(s, 0, keepdims=True)
                e = jnp.exp(s - peak)
                total = jnp.sum(e, 0, keepdims=True)
                lse_ref[g * GROUP + head, :, first:limit] = peak + jnp.log(total)
                probs.append((e * (1.0 / total)).astype(BF))
            prob = jnp.concatenate(probs, 1)
            out = dot_0(prob, v_ref[g, :limit, :])
            o_s[pl.ds(g * GROUP, GROUP), first:limit, :] = out.reshape(GROUP, Q_BLOCK, HEAD_SIZE)
        return 0

    lax.fori_loop(0, KEY_VALUE_HEADS, group, 0)
    for head in range(0, QUERY_HEADS - 1, 2):
        att_ref[:, head * 64 : head * 64 + 128] = jnp.concatenate([o_s[head], o_s[head + 1]], 1).astype(BF)
    att_ref[:, 512:576] = o_s[8].astype(BF)


def attention_backward(
    q_ref, k_ref, v_ref, lse_ref, att_ref, datt_ref, cos_ref, sin_ref, start_ref, out_ref,
    bias, do_s, delta_s, dqk_s, dv_s,
):
    tokens = att_ref.shape[0]
    fill_bias(bias, start_ref)
    ones = jnp.ones((8, HEAD_SIZE), BF)
    for head in range(QUERY_HEADS):
        cols = slice(head * 64, head * 64 + 64)
        grad = datt_ref[:, cols]
        do_s[head] = grad
        product = (grad.astype(F32) * att_ref[:, cols].astype(F32)).astype(BF)
        delta_s[head] = dot_t(ones, product)
    dqk_s[QUERY_HEADS:] = jnp.zeros((KEY_VALUE_HEADS, tokens, HEAD_SIZE), F32)
    dv_s[...] = jnp.zeros_like(dv_s)

    def group(g, _):
        for first in range(0, tokens, Q_BLOCK):
            limit = first + Q_BLOCK
            heads = pl.ds(g * GROUP, GROUP)
            queries = q_ref[heads, first:limit, :].reshape(GROUP * Q_BLOCK, HEAD_SIZE)
            grads = do_s[heads, first:limit, :].reshape(GROUP * Q_BLOCK, HEAD_SIZE)
            keys = k_ref[g, :limit, :]
            scores = dot_t(keys, queries)
            dprob = dot_t(v_ref[g, :limit, :], grads)
            mask = bias[:limit, first:limit]
            probs, dscores = [], []
            for head in range(GROUP):
                cols = slice(head * Q_BLOCK, (head + 1) * Q_BLOCK)
                lse = lse_ref[g * GROUP + head, :, first:limit]
                delta = delta_s[g * GROUP + head, 0:1, first:limit]
                p = jnp.exp(scores[:, cols] + mask - lse)
                probs.append(p.astype(BF))
                dscores.append((p * (dprob[:, cols] - delta)).astype(BF))
            prob = jnp.concatenate(probs, 1)
            dscore = jnp.concatenate(dscores, 1)
            dv_s[g, :limit, :] += jnp.dot(prob, grads, preferred_element_type=F32)
            dqk_s[QUERY_HEADS + g, :limit, :] += jnp.dot(dscore, queries, preferred_element_type=F32)
            dq = dot_0(dscore, keys) * HEAD_SIZE ** (-0.5)
            dqk_s[heads, first:limit, :] = dq.reshape(GROUP, Q_BLOCK, HEAD_SIZE)
        return 0

    lax.fori_loop(0, KEY_VALUE_HEADS, group, 0)
    cosine, sine = cos_ref[...], sin_ref[...]
    for chunk in range(6):
        x = jnp.concatenate([dqk_s[chunk * 2], dqk_s[chunk * 2 + 1]], 1)
        x = x * cosine - turned(x) * sine
        out_ref[:, chunk * 128 : chunk * 128 + 128] = x.astype(BF)
    out_ref[:, 768:896] = jnp.concatenate([dv_s[0], dv_s[1]], 1).astype(BF)
    out_ref[:, 896:960] = dv_s[2].astype(BF)


def vmem(count):
    return [pl.BlockSpec(memory_space=pltpu.VMEM)] * count


def run_forward(qkv, cosine, sine, start):
    tokens = qkv.shape[0]
    shape = jax.ShapeDtypeStruct
    return pl.pallas_call(
        attention_forward,
        out_shape=(
            shape((tokens, 576), BF),
            shape((QUERY_HEADS, tokens, HEAD_SIZE), BF),
            shape((KEY_VALUE_HEADS, tokens, HEAD_SIZE), BF),
            shape((KEY_VALUE_HEADS, tokens, HEAD_SIZE), BF),
            shape((QUERY_HEADS, 1, tokens), F32),
        ),
        in_specs=vmem(4),
        out_specs=tuple(vmem(5)),
        scratch_shapes=[
            pltpu.VMEM((tokens, tokens), F32),
            pltpu.VMEM((QUERY_HEADS, tokens, HEAD_SIZE), F32),
        ],
        compiler_params=pltpu.CompilerParams(vmem_limit_bytes=LIMIT),
        cost_estimate=pl.CostEstimate(flops=6 * 10**9, bytes_accessed=6 * 10**6, transcendentals=4 * 10**6),
        name="attention_forward",
    )(qkv, cosine, sine, start)


def run_backward(q, k, v, lse, att, datt, cosine, sine, start):
    tokens = att.shape[0]
    return pl.pallas_call(
        attention_backward,
        out_shape=jax.ShapeDtypeStruct((tokens, 960), BF),
        in_specs=vmem(9),
        out_specs=vmem(1)[0],
        scratch_shapes=[
            pltpu.VMEM((tokens, tokens), F32),
            pltpu.VMEM((QUERY_HEADS, tokens, HEAD_SIZE), BF),
            pltpu.VMEM((QUERY_HEADS, 8, tokens), F32),
            pltpu.VMEM((QUERY_HEADS + KEY_VALUE_HEADS, tokens, HEAD_SIZE), F32),
            pltpu.VMEM((KEY_VALUE_HEADS, tokens, HEAD_SIZE), F32),
        ],
        compiler_params=pltpu.CompilerParams(vmem_limit_bytes=LIMIT),
        cost_estimate=pl.CostEstimate(flops=12 * 10**9, bytes_accessed=7 * 10**6, transcendentals=4 * 10**6),
        name="attention_backward",
    )(q, k, v, lse, att, datt, cosine, sine, start)


def dot(a, b):
    return jnp.dot(a, b, preferred_element_type=F32)


def forward_layer(hidden_in, weights, tables):
    gain_one, w_qkv, w_o, gain_two, w_gu, w_d = weights
    scale_in = lax.rsqrt(jnp.mean(hidden_in * hidden_in, -1, keepdims=True) + EPS)
    normed = (hidden_in * scale_in * gain_one).astype(BF)
    qkv = dot(normed, w_qkv)
    attended, q, k, v, lse = run_forward(qkv, *tables)
    mixed = hidden_in + dot(attended, w_o)
    scale_mid = lax.rsqrt(jnp.mean(mixed * mixed, -1, keepdims=True) + EPS)
    normed_two = (mixed * scale_mid * gain_two).astype(BF)
    gateup = dot(normed_two, w_gu)
    inner = (jax.nn.silu(gateup[:, :FF]) * gateup[:, FF:]).astype(BF)
    result = mixed + dot(inner, w_d)
    return result, (hidden_in, scale_in, normed, q, k, v, lse, attended, mixed, scale_mid, normed_two, gateup, inner)


def backward_layer(grad_result, weights, tables, kept):
    gain_one, w_qkv, w_o, gain_two, w_gu, w_d = weights
    hidden_in, scale_in, normed, q, k, v, lse, attended, mixed, scale_mid, normed_two, gateup, inner = kept
    grad_low = grad_result.astype(BF)
    grad_wd = dot_0(inner, grad_low).astype(BF)
    grad_inner = dot_t(grad_low, w_d)
    gate = gateup[:, :FF]
    upper = gateup[:, FF:]
    sigma = jax.nn.sigmoid(gate)
    slope = sigma * (1.0 + gate * (1.0 - sigma))
    grad_gateup = jnp.concatenate([grad_inner * upper * slope, grad_inner * gate * sigma], 1).astype(BF)
    grad_wgu = dot_0(normed_two, grad_gateup).astype(BF)
    grad_normed_two = dot_t(grad_gateup, w_gu)
    grad_gain_two = jnp.sum(grad_normed_two * mixed * scale_mid, 0)
    weighted_two = grad_normed_two * gain_two
    grad_mixed = (
        grad_result
        + scale_mid * weighted_two
        - mixed * scale_mid**3 * jnp.mean(weighted_two * mixed, -1, keepdims=True)
    )
    grad_branch = grad_mixed.astype(BF)
    grad_wo = dot_0(attended, grad_branch).astype(BF)
    grad_att = dot_t(grad_branch, w_o).astype(BF)
    grad_qkv = run_backward(q, k, v, lse, attended, grad_att, *tables)
    grad_wqkv = dot_0(normed, grad_qkv).astype(BF)
    grad_normed = dot_t(grad_qkv, w_qkv)
    grad_gain_one = jnp.sum(grad_normed * hidden_in * scale_in, 0)
    weighted_one = grad_normed * gain_one
    grad_input = (
        grad_mixed
        + scale_in * weighted_one
        - hidden_in * scale_in**3 * jnp.mean(weighted_one * hidden_in, -1, keepdims=True)
    )
    return grad_input, (grad_gain_one, grad_wqkv, grad_wo, grad_gain_two, grad_wgu, grad_wd)


BOTH = ("section", "fsdp")


def gather(w):
    full = lax.all_gather(w[0], BOTH, axis=0, tiled=True)
    return full.reshape(2, full.shape[0] // 2, full.shape[1])


def reduce(first, second):
    both = jnp.concatenate([first, second], 0)
    part = lax.psum_scatter(both, BOTH, scatter_dimension=0, tiled=True)
    return lax.psum(part, "replica").astype(F32)[None]


def exchange(section, own_first, own_second):
    at_first = section == 0
    got = lax.ppermute(jnp.where(at_first, own_second, own_first), "section", [(0, 1), (1, 0)])
    keep = jnp.where(at_first, own_first, own_second)
    return jnp.where(at_first, jnp.concatenate([keep, got], 0), jnp.concatenate([got, keep], 0))


def shards(inputs, cotangent, seq_lengths, attn_gain, w_query, key_value_weight, w_out, ffn_gain, w_gateup, w_down):
    section = lax.axis_index("section")
    tokens = inputs.shape[0] // MICRO
    own = lambda array, count: lax.dynamic_slice_in_dim(array, section * count, count, 0)
    gains = gather(jnp.stack([attn_gain[0], ffn_gain[0]], 1)[None])
    qkv_full = gather(jnp.concatenate([w_query, key_value_weight], 2))
    out_full, gateup_full, down_full = gather(w_out), gather(w_gateup), gather(w_down)
    weights = [
        (gains[i, :, 0], qkv_full[i], out_full[i], gains[i, :, 1], gateup_full[i], down_full[i])
        for i in range(2)
    ]
    start, place = positions(own(seq_lengths, 1)[0], tokens)
    tables = rope_tables(place) + (start[None, :],)
    x = own(inputs, tokens)
    cot = own(cotangent, tokens)
    out_one, kept_one = forward_layer(x.astype(F32), weights[0], tables)
    middle = out_one.astype(BF)
    out_two, kept_two = forward_layer(middle.astype(F32), weights[1], tables)
    acts = exchange(section, middle, out_two.astype(BF))
    grad_two, grads_two = backward_layer(cot.astype(F32), weights[1], tables, kept_two)
    low_two = grad_two.astype(BF)
    grad_one, grads_one = backward_layer(low_two.astype(F32), weights[0], tables, kept_one)
    in_grads = exchange(section, grad_one.astype(BF), low_two).astype(F32)
    gain_pair = [jnp.stack([g[0], g[3]], 1).astype(BF) for g in (grads_one, grads_two)]
    gain_sum = reduce(*gain_pair)
    qkv_sum = reduce(grads_one[1], grads_two[1])
    out_sum = reduce(grads_one[2], grads_two[2])
    gateup_sum = reduce(grads_one[4], grads_two[4])
    down_sum = reduce(grads_one[5], grads_two[5])
    return (
        acts[None],
        in_grads[None],
        gain_sum[:, :, 0],
        qkv_sum[:, :, :576],
        qkv_sum[:, :, 576:],
        out_sum,
        gain_sum[:, :, 1],
        gateup_sum,
        down_sum,
    )


def solution(mesh):
    return jax.shard_map(
        shards,
        mesh=mesh,
        in_specs=(
            P(("fsdp", "replica"), None),
            P(("fsdp", "replica"), None),
            P(("fsdp", "replica"), None),
            P("section", "fsdp"),
            P("section", "fsdp", None),
            P("section", "fsdp", None),
            P("section", "fsdp", None),
            P("section", "fsdp"),
            P("section", "fsdp", None),
            P("section", "fsdp", None),
        ),
        out_specs=(
            P("section", ("fsdp", "replica"), None),
            P("section", ("fsdp", "replica"), None),
            P("section", "fsdp"),
            P("section", "fsdp", None),
            P("section", "fsdp", None),
            P("section", "fsdp", None),
            P("section", "fsdp"),
            P("section", "fsdp", None),
            P("section", "fsdp", None),
        ),
        check_vma=False,
    )
```

time: 699 us -> 593 us (0.85)
  waiting for transfers between devices: 148 us -> 327 us
  matrix products: 266 us -> 90 us
  other arithmetic: 111 us -> 32.9 us
  Pallas kernels: 0 us -> 65.4 us
  blocking collectives: 71.6 us -> 26.7 us
  local copies, waits for them, and re-layouts: 68.9 us -> 29.1 us
    dot_general x87 -> x24, matrix products: 266 us -> 90 us  [the longest x8 34.3 us: dot(): return jnp.dot(a, b, preferred_element_type=F32)]
    all_gather x2 -> x4, waiting for transfers between devices: 0.02 us -> 92.1 us  [gather(): full = lax.all_gather(w[0], BOTH, axis=0, tiled=True)]
    pallas_call x0 -> x4, Pallas kernels: none -> 65.4 us  [the longest x2 36.6 us: run_backward(): pl.pallas_call(attention_backward, out_shape=jax.ShapeDtypeStruct((tokens...]
    reduce_scatter x1 -> x2, waiting for transfers between devices: 51.2 us -> 113 us  [reduce(): part = lax.psum_scatter(both, BOTH, scatter_dimension=0, tiled=True)]
    convert_element_type x31 -> x5, other arithmetic: 53.6 us -> 5.17 us  [the longest x1 2.37 us: shards(): in_grads = exchange(section, grad_one.astype(BF), low_two).astype(F32)]
    unnamed x553 -> x115, local copies, waits for them, and re-layouts: 56.2 us -> 21.7 us
    all_gather x3 -> x1, blocking collectives: 39.7 us -> 14.9 us  [gather(): full = lax.all_gather(w[0], BOTH, axis=0, tiled=True)]
    psum x1, waiting for transfers between devices: 43.6 us -> 66.2 us  [reduce(): return lax.psum(part, 'replica').astype(F32)[None]]
  transfers between devices with their start and end apart: 12 -> 12, of which waited for: 4 -> 9; matrix products, arithmetic and copies ran while one was open for 24% -> 14% of each run, Pallas kernels for 0% -> 6%
where the time goes in v1:
time: 593 us; the launch traced here: 587 us
  waiting for transfers between devices  327 us (55%)
  matrix products  90 us (15%)
  Pallas kernels  65.4 us (11%)
  other arithmetic  32.9 us (6%)
  local copies, waits for them, and re-layouts  29.1 us (5%)
  blocking collectives  26.7 us (5%)
  between operations  15.2 us (3%)
    reduce_scatter x2, waiting for transfers between devices, reduce(): part = lax.psum_scatter(both, BOTH, scatter_dimension=0, tiled=True)  113 us
    all_gather x4, waiting for transfers between devices, gather(): full = lax.all_gather(w[0], BOTH, axis=0, tiled=True)  92.1 us
    psum x1, waiting for transfers between devices, reduce(): return lax.psum(part, 'replica').astype(F32)[None]  66.2 us
    unnamed x13, waiting for transfers between devices  55.5 us
    pallas_call x2, Pallas kernels, run_backward(): pl.pallas_call(attention_backward, out_shape=jax.ShapeDtypeStruct((tokens...  36.6 us
    dot_general x8, matrix products, dot(): return jnp.dot(a, b, preferred_element_type=F32)  34.3 us
    dot_general x8, matrix products, dot_t(): lax.dot_general(a, b, (((1,), (1,)), ((), ())), preferred_element_type=F32)  31.5 us
    pallas_call x2, Pallas kernels, run_forward(): pl.pallas_call(attention_forward, out_shape=(shape((tokens, 576), BF), sh...  28.7 us
  transfers between devices with their start and end apart: 12, of which 9 were waited for; matrix products, arithmetic and copies ran while one was open for 14% of the time, Pallas kernels for 6%

profile of v1, /device:TPU:0, one launch (start us, length us, event | category | flops | bytes accessed | tf_op | source)
XLA Modules:
  0.0 587.5 jit_solution(12313245816450493961)
XLA Ops:
  12.2 14.9 %all-gather.4 = bf16[8,144,2]{1,2,0:T(2,128)(2,1)S(1)} all-gather(bf16[1,144,2]{1,2,0:T(2,128)(2,1)S(1)} %maximum_bitcast_fusion), channel_id=1, replica_groups=mesh['section'=2,'fsdp'=4,'replica'=4] {'section','fsdp'}, dimensions={0}, use_global_device_ids=true | all-gather | bytes 5184 | tf_op jit(solution)/shard_map/all_gather | solution.py:268
  31.7 10.6 %all-gather.10.cloned.1.call-done = bf16[1,1152,960]{2,1,0:T(8,128)(2,1)} async-done(((bf16[1,144,960]{2,1,0:T(8,128)(2,1)}), bf16[1,1152,960]{2,1,0:T(8,128)(2,1)}) %all-gather.10.cloned.1.call-update) | async-done | bytes 2211856 | tf_op jit(solution)/shard_map/all_gather | solution.py:268
  46.7 14.5 %attention_forward.2 = (bf16[768,576]{1,0:T(8,128)(2,1)}, bf16[9,768,64]{2,1,0:T(8,128)(2,1)}, bf16[3,768,64]{2,1,0:T(8,128)(2,1)}, bf16[3,768,64]{2,1,0:T(8,128)(2,1)}, f32[9,1,768]{2,1,0:T(1,128)}) custom-call(f32[768,960]{1,0:T(8,128)} %fusion.28.qkv_ref, f32[768,128]{1,0:T(8,128)} %get-tuple-element.133.cos_ref, f32[768,128]{1,0:T(8,128)} %get-tuple-element.134.sin_ref, ...), custom_call_target="tpu_custom_call" | custom-call | flops 6000000000 | bytes 6000000 | tf_op jit(solution)/shard_map/attention_forward/pallas_call | solution.py:168
  61.3 8.2 %all-gather.12.cloned.1.call-done = bf16[1,1152,576]{2,1,0:T(8,128)(2,1)} async-done(((bf16[1,144,576]{2,1,0:T(8,128)(2,1)}), bf16[1,1152,576]{2,1,0:T(8,128)(2,1)}) %all-gather.12.cloned.1.call-update) | async-done | bytes 1327120 | tf_op jit(solution)/shard_map/all_gather | solution.py:268
  71.9 48.4 %all-gather.14.cloned.1.call-done = bf16[1,1152,3072]{2,1,0:T(8,128)(2,1)} async-done(((bf16[1,144,3072]{2,1,0:T(8,128)(2,1)}), bf16[1,1152,3072]{2,1,0:T(8,128)(2,1)}) %all-gather.14.cloned.1.call-update) | async-done | bytes 7077904 | tf_op jit(solution)/shard_map/all_gather | solution.py:268
  120.3 6.0 %fusion.1 = f32[768,3072]{1,0:T(8,128)S(1)} fusion(bf16[1,1152,3072]{2,1,0:T(8,128)(2,1)} %all-gather.14.cloned.1.call-done, f32[768,576]{0,1:T(8,128)S(1)} %get-tuple-element.124, f32[576]{0:T(1024)S(1)} %get-tuple-element.93, f32[768]{0:T(1024)S(1)} %get-tuple-element.114), kind=kOutput, calls=%fused_computation.29 | convolution fusion | flops 2719236096 | bytes 14750976 | tf_op jit(solution)/shard_map/dot_general | solution.py:210
  131.6 24.9 %all-gather.16.cloned.1.call-done = bf16[1,3072,576]{1,2,0:T(8,128)(2,1)} async-done(((bf16[1,384,576]{1,2,0:T(8,128)(2,1)}), bf16[1,3072,576]{1,2,0:T(8,128)(2,1)}) %all-gather.16.cloned.1.call-update) | async-done | bytes 3538960 | tf_op jit(solution)/shard_map/all_gather | solution.py:268
  164.2 14.2 %attention_forward.3 = (bf16[768,576]{1,0:T(8,128)(2,1)}, bf16[9,768,64]{2,1,0:T(8,128)(2,1)}, bf16[3,768,64]{2,1,0:T(8,128)(2,1)}, bf16[3,768,64]{2,1,0:T(8,128)(2,1)}, f32[9,1,768]{2,1,0:T(1,128)}) custom-call(f32[768,960]{1,0:T(8,128)} %fusion.30.qkv_ref, f32[768,128]{1,0:T(8,128)} %get-tuple-element.133.cos_ref, f32[768,128]{1,0:T(8,128)} %get-tuple-element.134.sin_ref, ...), custom_call_target="tpu_custom_call" | custom-call | flops 6000000000 | bytes 6000000 | tf_op jit(solution)/shard_map/attention_forward/pallas_call | solution.py:168
  180.7 6.7 %fusion.3 = f32[768,3072]{1,0:T(8,128)S(1)} fusion(bf16[1,1152,3072]{2,1,0:T(8,128)(2,1)} %all-gather.14.cloned.1.call-done, f32[768,576]{0,1:T(8,128)S(1)} %get-tuple-element.128, f32[576]{0:T(1024)S(1)} %copy-done.24, f32[768]{0:T(1024)S(1)} %get-tuple-element.118), kind=kOutput, calls=%fused_computation.31 | convolution fusion | flops 2719236096 | bytes 14750976 | tf_op jit(solution)/shard_map/dot_general | solution.py:210
  187.4 6.3 %multiply_convert_fusion.3 = (bf16[768,1536]{1,0:T(8,128)(2,1)}, bf16[768,1536]{1,0:T(8,128)(2,1)}, bf16[768,1536]{1,0:T(8,128)(2,1)}) fusion(f32[768,3072]{1,0:T(8,128)S(1)} %fusion.3, bf16[1,3072,576]{1,2,0:T(8,128)(2,1)S(1)} %copy-done.38, bf16[1536,576]{0,1:T(8,128)(2,1)S(1)} %copy-done.16, s32[]{:T(128)S(6)} %select_n.59), kind=kOutput, calls=%fused_computation.6 | convolution fusion | flops 1377828864 | bytes 19169284 | tf_op jit(solution)/shard_map/dot_general | solution.py:60
  193.7 6.1 %multiply_reduce_fusion = (bf16[576]{0:T(1024)(128)(2,1)}, f32[768]{0:T(1024)S(1)}, f32[768,576]{0,1:T(8,128)S(1)}) fusion(f32[768,576]{0,1:T(8,128)S(1)} %get-tuple-element.128, f32[768]{0:T(1024)S(1)} %get-tuple-element.118, f32[576]{0:T(1024)S(1)} %copy-done.24, bf16[1,1152,3072]{2,1,0:T(8,128)(2,1)S(1)} %bitcast.109, ...), kind=kOutput, calls=%fused_computation.58 | convolution fusion | flops 2729999104 | bytes 11808896 | tf_op jit(solution)/shard_map/dot_general | solution.py:60
  204.9 18.4 %attention_backward.2 = bf16[768,960]{1,0:T(8,128)(2,1)} custom-call(bf16[9,768,64]{2,1,0:T(8,128)(2,1)} %get-tuple-element.21.q_ref, bf16[3,768,64]{2,1,0:T(8,128)(2,1)} %get-tuple-element.22.k_ref, bf16[3,768,64]{2,1,0:T(8,128)(2,1)} %get-tuple-element.23.v_ref, f32[9,1,768]{2,1,0:T(1,128)} %get-tuple-element.24.lse_ref, ...), custom_call_target="tpu_custom_call" | custom-call | flops 12000000000 | bytes 7000000 | tf_op jit(solution)/shard_map/attention_backward/pallas_call | solution.py:191
  227.8 6.2 %multiply_convert_fusion.1 = (bf16[768,1536]{1,0:T(8,128)(2,1)S(1)}, bf16[768,1536]{1,0:T(8,128)(2,1)S(1)}) fusion(f32[768,3072]{1,0:T(8,128)} %copy-done, bf16[768,576]{0,1:T(8,128)(2,1)S(1)} %fusion.18, bf16[1,3072,576]{1,2,0:T(8,128)(2,1)S(1)} %copy-done.39), kind=kOutput, calls=%fused_computation.4 | convolution fusion | flops 1374289920 | bytes 16809984 | tf_op jit(solution)/shard_map/dot_general | solution.py:60
  251.8 6.2 %copy.60 = bf16[3072,576]{1,0:T(8,128)(2,1)} copy(bf16[3072,576]{0,1:T(8,128)(2,1)} %pad_maximum_fusion.3) | data formatting | bytes 7077888
  261.6 18.2 %attention_backward.3 = bf16[768,960]{1,0:T(8,128)(2,1)} custom-call(bf16[9,768,64]{2,1,0:T(8,128)(2,1)} %get-tuple-element.25.q_ref, bf16[3,768,64]{2,1,0:T(8,128)(2,1)} %get-tuple-element.26.k_ref, bf16[3,768,64]{2,1,0:T(8,128)(2,1)} %get-tuple-element.27.v_ref, f32[9,1,768]{2,1,0:T(1,128)} %get-tuple-element.28.lse_ref, ...), custom_call_target="tpu_custom_call" | custom-call | flops 12000000000 | bytes 7000000 | tf_op jit(solution)/shard_map/attention_backward/pallas_call | solution.py:191
  285.7 7.8 %convolution_convert_fusion = bf16[576,3072]{1,0:T(8,128)(2,1)} fusion(bf16[768,1536]{1,0:T(8,128)(2,1)} %get-tuple-element.104, bf16[768,1536]{1,0:T(8,128)(2,1)} %get-tuple-element.103, f32[768,576]{0,1:T(8,128)} %copy-done.6, f32[576]{0:T(1024)} %get-tuple-element.91, f32[768]{0:T(1024)S(1)} %get-tuple-element.118), kind=kOutput, calls=%fused_computation.11 | convolution fusion | flops 2730442752 | bytes 10032384 | tf_op jit(solution)/shard_map/dot_general | solution.py:64
  298.4 6.6 %pad_maximum_fusion = bf16[1152,3072]{1,0:T(8,128)(2,1)} fusion(bf16[576,3072]{1,0:T(8,128)(2,1)} %convolution_convert_fusion, bf16[576,3072]{1,0:T(8,128)(2,1)} %convolution_convert_fusion.1), kind=kLoop, calls=%fused_computation | loop fusion | flops 14155776 | bytes 14155776 | tf_op jit(solution)/shard_map/concatenate | solution.py:273
  305.2 5.6 select_bitcast_fusion.1
  316.6 19.5 %reduce-scatter.20.cloned.1.call-done = bf16[384,576]{1,0:T(8,128)(2,1)} async-done(((bf16[3072,576]{1,0:T(8,128)(2,1)}), bf16[384,576]{1,0:T(8,128)(2,1)}) %reduce-scatter.20.cloned.1.call-update) | async-done | bytes 442384
  338.0 43.9 %reduce-scatter.12.cloned.1.call-done = bf16[144,960]{1,0:T(8,128)(2,1)} async-done(((bf16[1152,960]{1,0:T(8,128)(2,1)}), bf16[144,960]{1,0:T(8,128)(2,1)}) %reduce-scatter.12.cloned.1.call-update) | async-done | bytes 276496 | tf_op jit(solution)/shard_map/reduce_scatter | solution.py:274
  381.9 69.4 %reduce-scatter.14.cloned.1.call-done = bf16[144,3072]{1,0:T(8,128)(2,1)} async-done(((bf16[1152,3072]{1,0:T(8,128)(2,1)}), bf16[144,3072]{1,0:T(8,128)(2,1)}) %reduce-scatter.14.cloned.1.call-update) | async-done | bytes 884752 | tf_op jit(solution)/shard_map/reduce_scatter | solution.py:274
  454.0 34.0 %reduce-scatter.16.cloned.1.call-done = bf16[144,2]{1,0:T(8,128)(2,1)} async-done(((bf16[1152,2]{1,0:T(8,128)(2,1)}), bf16[144,2]{1,0:T(8,128)(2,1)}) %reduce-scatter.16.cloned.1.call-update) | async-done | bytes 592
  488.8 11.8 %psum.35 = bf16[1,144,2]{1,2,0:T(2,128)(2,1)S(1)} all-reduce(bf16[1,144,2]{1,2,0:T(2,128)(2,1)S(1)} %bitcast.104), channel_id=1, replica_groups=mesh['section'=2,'fsdp'=4,'replica'=4] {'replica'}, use_global_device_ids=true, to_apply=%region_15.16 | all-reduce | flops 288 | bytes 1152 | tf_op jit(solution)/shard_map/psum | solution.py:275
  506.6 66.2 %all-reduce.3.cloned.1.call-done = (bf16[1,144,960]{2,1,0:T(8,128)(2,1)}, bf16[1,144,576]{1,2,0:T(8,128)(2,1)}, bf16[1,144,3072]{2,1,0:T(8,128)(2,1)}, bf16[1,384,576]{1,2,0:T(8,128)(2,1)}) async-done(((bf16[1,144,960]{2,1,0:T(8,128)(2,1)}, bf16[1,144,576]{1,2,0:T(8,128)(2,1)}, bf16[1,144,3072]{2,1,0:T(8,128)(2,1)}, bf16[1,384,576]{1,2,0:T(8,128)(2,1)}), (bf16[1,144,960]{2,1,0:T(8,128)(2,1)}, ...) | async-done | bytes 1769488 | tf_op jit(solution)/shard_map/psum | solution.py:275
  (204 shorter events, 97.6 us)
Async XLA Ops:
  7.2 20.0 %copy-start.7 = (bf16[1536,576]{0,1:T(8,128)(2,1)S(1)}, bf16[1536,576]{0,1:T(8,128)(2,1)}, u32[]{:S(2)}) copy-start(bf16[1536,576]{0,1:T(8,128)(2,1)} %param.10) | copy-start | bytes 5308420
  7.2 35.0 %all-gather.10.cloned.1.call-start = ((), (), s32[]{:S(2)}) async-start(), calls=%async_computation.7 | async-start | bytes 2654208 | tf_op jit(solution)/shard_map/all_gather | solution.py:268
  9.2 60.3 %all-gather.12.cloned.1.call-start = ((), (), s32[]{:S(2)}) async-start(), calls=%async_computation.8 | async-start | bytes 1658880 | tf_op jit(solution)/shard_map/all_gather | solution.py:268
  10.0 110.3 %all-gather.14.cloned.1.call-start = ((), (), s32[]{:S(2)}) async-start(), calls=%async_computation.9 | async-start | bytes 7962624 | tf_op jit(solution)/shard_map/all_gather | solution.py:268
  10.7 145.8 %all-gather.16.cloned.1.call-start = ((), (), s32[]{:S(2)}) async-start(), calls=%async_computation.10 | async-start | bytes 3981312 | tf_op jit(solution)/shard_map/all_gather | solution.py:268
  11.3 303.5 %reduce-scatter.18.cloned.1.call-start = ((), (), s32[]{:S(2)}) async-start(), calls=%async_computation.12 | async-start | bytes 1658880
  28.1 18.6 %copy-start.19 = (f32[576]{0:T(1024)}, f32[576]{0:T(1024)S(1)}, u32[]{:S(2)}) copy-start(f32[576]{0:T(1024)S(1)} %get-tuple-element.94) | copy-start | bytes 6916
  28.1 92.2 %copy-start.21 = (f32[576]{0:T(1024)}, f32[576]{0:T(1024)S(1)}, u32[]{:S(2)}) copy-start(f32[576]{0:T(1024)S(1)} %get-tuple-element.93) | copy-start | bytes 6916
  71.8 48.4 %copy-start.3 = (f32[768,576]{0,1:T(8,128)}, f32[768,576]{0,1:T(8,128)S(1)}, u32[]{:S(2)}) copy-start(f32[768,576]{0,1:T(8,128)S(1)} %get-tuple-element.124) | copy-start | bytes 5308420
  131.6 28.7 %copy-start.1 = (bf16[768,1536]{1,0:T(8,128)(2,1)}, bf16[768,1536]{1,0:T(8,128)(2,1)S(1)}, u32[]{:S(2)}) copy-start(bf16[768,1536]{1,0:T(8,128)(2,1)S(1)} %multiply_convert_fusion.5) | copy-start | bytes 7077892
  131.6 29.4 %copy-start.29 = (f32[576]{0:T(1024)S(1)}, f32[576]{0:T(1024)}, u32[]{:S(2)}) copy-start(f32[576]{0:T(1024)} %get-tuple-element.92) | copy-start | bytes 6916
  160.3 67.0 %copy-start.13 = (bf16[768,576]{0,1:T(8,128)(2,1)}, bf16[768,576]{0,1:T(8,128)(2,1)S(1)}, u32[]{:S(2)}) copy-start(bf16[768,576]{0,1:T(8,128)(2,1)S(1)} %get-tuple-element.126) | copy-start | bytes 2654212
  180.6 19.2 %copy-start.6 = (f32[768,576]{0,1:T(8,128)}, f32[768,576]{0,1:T(8,128)S(1)}, u32[]{:S(2)}) copy-start(f32[768,576]{0,1:T(8,128)S(1)} %get-tuple-element.128) | copy-start | bytes 5308420
  204.9 18.5 %copy-start.26 = (f32[768]{0:T(1024)S(1)}, f32[768]{0:T(1024)}, u32[]{:S(2)}) copy-start(f32[768]{0:T(1024)} %copy-done.25) | copy-start | bytes 9220
  204.9 18.5 %copy-start.30 = (f32[576]{0:T(1024)S(1)}, f32[576]{0:T(1024)}, u32[]{:S(2)}) copy-start(f32[576]{0:T(1024)} %get-tuple-element.92) | copy-start | bytes 6916
  244.3 91.8 %reduce-scatter.20.cloned.1.call-start = ((), (), s32[]{:S(2)}) async-start(), calls=%async_computation.13 | async-start | bytes 4423680
  258.1 123.8 %reduce-scatter.12.cloned.1.call-start = ((), (), s32[]{:S(2)}) async-start(), calls=%async_computation.5 | async-start | bytes 2654208 | tf_op jit(solution)/shard_map/reduce_scatter | solution.py:274
  285.4 165.9 %reduce-scatter.14.cloned.1.call-start = ((), (), s32[]{:S(2)}) async-start(), calls=%async_computation.6 | async-start | bytes 7962624 | tf_op jit(solution)/shard_map/reduce_scatter | solution.py:274
  305.0 182.9 %reduce-scatter.16.cloned.1.call-start = ((), (), s32[]{:S(2)}) async-start(), calls=%async_computation.11 | async-start | bytes 331776
  310.8 190.4 %collective-permute-start = (bf16[768,576]{0,1:T(8,128)(2,1)}, bf16[768,576]{0,1:T(8,128)(2,1)}, u32[]{:S(2)}, u32[]{:S(2)}) collective-permute-start(bf16[768,576]{0,1:T(8,128)(2,1)} %get-tuple-element.107), channel_id=1, source_target_pairs={{0,16},{16,0},{1,17},{17,1},{2,18},{18,2},{3,19},{19,3},{4,20},{20... | collective-permute-start | bytes 2654216 | tf_op jit(solution)/shard_map/ppermute | solution.py:280
  314.7 136.7 %copy-start.18 = (f32[768]{0:T(1024)S(1)}, f32[768]{0:T(1024)}, u32[]{:S(2)}) copy-start(f32[768]{0:T(1024)} %get-tuple-element.111) | copy-start | bytes 9220
  314.7 258.0 %all-reduce.3.cloned.1.call-start = ((), (), s32[]{:S(2)}) async-start(), calls=%async_computation.14 | async-start | bytes 3833856 | tf_op jit(solution)/shard_map/psum | solution.py:275
  453.8 47.4 %copy-start.11 = (bf16[1,768,576]{1,2,0:T(8,128)(2,1)S(1)}, bf16[1,768,576]{1,2,0:T(8,128)(2,1)}, u32[]{:S(2)}) copy-start(bf16[1,768,576]{1,2,0:T(8,128)(2,1)} %get-tuple-element.106) | copy-start | bytes 2654212
  453.9 50.3 %collective-permute-start.1 = (bf16[768,576]{0,1:T(8,128)(2,1)S(1)}, bf16[768,576]{0,1:T(8,128)(2,1)S(1)}, u32[]{:S(2)}, u32[]{:S(2)}) collective-permute-start(bf16[768,576]{0,1:T(8,128)(2,1)S(1)} %broadcast_select_fusion), channel_id=1, source_target_pairs={{0,16},{16,0},{1,17},{17,1},{2,18},{18,2},{3,19},{19,3},{4,20},{20... | collective-permute-start | bytes 2654216 | tf_op jit(solution)/shard_map/ppermute | solution.py:280
  (42 other events, 249.7 us)
Sparse Core Ops, SparseCore 0:
  10.5 31.7 all-gather.9
  44.2 25.2 all-gather.11
  71.4 48.8 all-gather.13
  122.0 34.5 all-gather.15
  244.4 37.7 reduce-scatter.17
  286.0 50.0 reduce-scatter.19
  339.4 42.4 reduce-scatter.11
  385.8 65.4 reduce-scatter.13
  455.0 32.8 reduce-scatter.15
  491.0 81.6 all-reduce.2

commit v2 on v1

--- a/solution.py
+++ b/solution.py
@@ -261,18 +261,102 @@
     return grad_input, (grad_gain_one, grad_wqkv, grad_wo, grad_gain_two, grad_wgu, grad_wd)
 
 
-BOTH = ("section", "fsdp")
-
-
-def gather(w):
-    full = lax.all_gather(w[0], BOTH, axis=0, tiled=True)
-    return full.reshape(2, full.shape[0] // 2, full.shape[1])
-
-
-def reduce(first, second):
-    both = jnp.concatenate([first, second], 0)
-    part = lax.psum_scatter(both, BOTH, scatter_dimension=0, tiled=True)
-    return lax.psum(part, "replica").astype(F32)[None]
+SWAP = [(0, 1), (1, 0)]
+
+
+def assemble_kernel(*refs):
+    pieces, full, sems = refs[:8], refs[8], refs[9]
+    section = lax.axis_index("section")
+    own = lax.axis_index("fsdp")
+    copies = []
+    for core in range(2):
+        half = (section + core) % 2
+        for step in range(4):
+            low = (own % 2 + step % 2) % 2
+            high = (own // 2 + step // 2) % 2
+            at = core * 4 + step
+            copies.append(pltpu.make_async_copy(pieces[at], full.at[high * 2 + low, half], sems.at[at]))
+    for copy in copies:
+        copy.start()
+    for copy in copies:
+        copy.wait()
+
+
+def assemble(pieces):
+    rows, columns = pieces[0].shape
+    full = pl.pallas_call(
+        assemble_kernel,
+        out_shape=jax.ShapeDtypeStruct((4, 2, rows, columns), BF),
+        in_specs=[pl.BlockSpec(memory_space=pl.ANY)] * 8,
+        out_specs=pl.BlockSpec(memory_space=pl.ANY),
+        scratch_shapes=[pltpu.SemaphoreType.DMA((8,))],
+        compiler_params=pltpu.CompilerParams(vmem_limit_bytes=LIMIT),
+        cost_estimate=pl.CostEstimate(flops=0, bytes_accessed=32 * rows * columns, transcendentals=0),
+        name="assemble",
+    )(*pieces)
+    return full.reshape(8 * rows, columns)
+
+
+def peer(value, step):
+    return lax.ppermute(value, "fsdp", [(i, i ^ step) for i in range(4)])
+
+
+def swap(value):
+    return lax.ppermute(value, "section", SWAP)
+
+
+def gather(section, packs):
+    at_first = section == 0
+    halves = [[], []]
+    for pack in packs:
+        parts = pack.reshape(2, pack.shape[0] // 2, pack.shape[1])
+        keep = jnp.where(at_first, parts[0], parts[1])
+        got = swap(jnp.where(at_first, parts[1], parts[0]))
+        halves[0].append(jnp.where(at_first, keep, got))
+        halves[1].append(jnp.where(at_first, got, keep))
+    order = halves[0] + halves[1]
+    arrived = []
+    full = []
+    for at, half in enumerate(order):
+        if at >= 2:
+            half = lax.optimization_barrier((half, arrived[at - 2]))[0]
+        pieces = [half] + [peer(half, step) for step in (3, 1, 2)]
+        pieces = [pieces[0], pieces[2], pieces[3], pieces[1]]
+        arrived.append(pieces[1:])
+        full.append(assemble(pieces + [swap(piece) for piece in pieces]))
+    return full[: len(packs)], full[len(packs) :]
+
+
+def replica_sum(own):
+    count = lax.axis_size("replica")
+    if count != 4:
+        return lax.psum(own.astype(BF), "replica").astype(F32)
+    send = lambda value, pairs: lax.ppermute(value.astype(BF), "replica", pairs).astype(F32)
+    one = send(own, [(0, 1), (3, 2)])
+    two = send(own + one, [(1, 2), (2, 1)])
+    three = send(own + two, [(2, 3), (1, 0)])
+    return own + one + two + three
+
+
+def reduce(section, grad):
+    own = lax.axis_index("fsdp")
+    rows, columns = grad.shape[0] // 8, grad.shape[1]
+    parts = grad.reshape(4, 2, rows, columns)
+    pick = lambda half: lax.dynamic_slice_in_dim(parts, half, 1, 1)[:, 0]
+    half = (pick(section).astype(F32) + swap(pick(1 - section)).astype(F32)).astype(BF)
+    block = lambda at: lax.dynamic_slice_in_dim(half, at, 1, 0)[0]
+    total = block(own).astype(F32)
+    for step in (3, 1, 2):
+        total = total + peer(block(own ^ step), step).astype(F32)
+    return replica_sum(total).astype(BF)
+
+
+def finish(section, first, second):
+    at_first = section == 0
+    got = swap(jnp.where(at_first, second, first))
+    keep = jnp.where(at_first, first, second)
+    low, high = jnp.where(at_first, keep, got), jnp.where(at_first, got, keep)
+    return jnp.concatenate([low, high], 0).astype(F32)[None]
 
 
 def exchange(section, own_first, own_second):
@@ -286,12 +370,13 @@
     section = lax.axis_index("section")
     tokens = inputs.shape[0] // MICRO
     own = lambda array, count: lax.dynamic_slice_in_dim(array, section * count, count, 0)
-    gains = gather(jnp.stack([attn_gain[0], ffn_gain[0]], 1)[None])
-    qkv_full = gather(jnp.concatenate([w_query, key_value_weight], 2))
-    out_full, gateup_full, down_full = gather(w_out), gather(w_gateup), gather(w_down)
+    pad = lambda rows: jnp.zeros((rows, 126), BF)
+    mixed_pack = jnp.concatenate(
+        [w_query[0], key_value_weight[0], w_out[0], attn_gain[0][:, None], ffn_gain[0][:, None], pad(w_out.shape[1])], 1
+    )
     weights = [
-        (gains[i, :, 0], qkv_full[i], out_full[i], gains[i, :, 1], gateup_full[i], down_full[i])
-        for i in range(2)
+        (a[:, 1536], a[:, :960], a[:, 960:1536], a[:, 1537], gu, down)
+        for a, gu, down in gather(section, [mixed_pack, w_gateup[0], w_down[0]])
     ]
     start, place = positions(own(seq_lengths, 1)[0], tokens)
     tables = rope_tables(place) + (start[None, :],)
@@ -305,20 +390,20 @@
     low_two = grad_two.astype(BF)
     grad_one, grads_one = backward_layer(low_two.astype(F32), weights[0], tables, kept_one)
     in_grads = exchange(section, grad_one.astype(BF), low_two).astype(F32)
-    gain_pair = [jnp.stack([g[0], g[3]], 1).astype(BF) for g in (grads_one, grads_two)]
-    gain_sum = reduce(*gain_pair)
-    qkv_sum = reduce(grads_one[1], grads_two[1])
-    out_sum = reduce(grads_one[2], grads_two[2])
-    gateup_sum = reduce(grads_one[4], grads_two[4])
-    down_sum = reduce(grads_one[5], grads_two[5])
+    sums = []
+    for gain_one, g_qkv, g_out, gain_two, g_gateup, g_down in (grads_two, grads_one):
+        gains = [gain_one.astype(BF)[:, None], gain_two.astype(BF)[:, None], pad(g_qkv.shape[0])]
+        mixed = jnp.concatenate([g_qkv, g_out] + gains, 1)
+        sums.append([reduce(section, g) for g in (g_down, g_gateup, mixed)])
+    down_sum, gateup_sum, mixed_sum = [finish(section, b, a) for a, b in zip(*sums)]
     return (
         acts[None],
         in_grads[None],
-        gain_sum[:, :, 0],
-        qkv_sum[:, :, :576],
-        qkv_sum[:, :, 576:],
-        out_sum,
-        gain_sum[:, :, 1],
+        mixed_sum[:, :, 1536],
+        mixed_sum[:, :, :576],
+        mixed_sum[:, :, 576:960],
+        mixed_sum[:, :, 960:1536],
+        mixed_sum[:, :, 1537],
         gateup_sum,
         down_sum,
     )

time: 593 us -> 931 us (1.57)
  Pallas kernels: 65.4 us -> 522 us
  waiting for transfers between devices: 327 us -> 127 us
  starting transfers between devices: 1.14 us -> 80.3 us
  local copies, waits for them, and re-layouts: 29.1 us -> 60 us
  blocking collectives: 26.7 us -> 0 us
  other arithmetic: 32.9 us -> 46.1 us
  between operations: 15.2 us -> 2.61 us
    pallas_call x0 -> x6, Pallas kernels: none -> 457 us  [assemble(): pl.pallas_call(assemble_kernel, out_shape=jax.ShapeDtypeStruct((4, 2, row...]
    ppermute x0 -> x90, waiting for transfers between devices: none -> 127 us  [the longest x36 71.8 us: peer(): return lax.ppermute(value, 'fsdp', [(i, i ^ step) for i in range(4)])]
    reduce_scatter x2 -> x0, waiting for transfers between devices: 113 us -> none  [reduce(): part = lax.psum_scatter(both, BOTH, scatter_dimension=0, tiled=True)]
    all_gather x4 -> x0, waiting for transfers between devices: 92.1 us -> none  [gather(): full = lax.all_gather(w[0], BOTH, axis=0, tiled=True)]
    ppermute x0 -> x90, starting transfers between devices: none -> 79.8 us  [the longest x36 45.5 us: peer(): return lax.ppermute(value, 'fsdp', [(i, i ^ step) for i in range(4)])]
    psum x1 -> x0, waiting for transfers between devices: 66.2 us -> none  [reduce(): return lax.psum(part, 'replica').astype(F32)[None]]
    unnamed x13 -> x0, waiting for transfers between devices: 55.5 us -> none
    all_gather x1 -> x0, blocking collectives: 14.9 us -> none  [gather(): full = lax.all_gather(w[0], BOTH, axis=0, tiled=True)]
  transfers between devices with their start and end apart: 12 -> 92, of which waited for: 9 -> 27; matrix products, arithmetic and copies ran while one was open for 14% -> 11% of each run, Pallas kernels for 6% -> 41%
where the time goes in v2:
time: 931 us; the launch traced here: 922 us
  Pallas kernels  522 us (56%)
  waiting for transfers between devices  127 us (14%)
  matrix products  84.1 us (9%)
  starting transfers between devices  80.3 us (9%)
  local copies, waits for them, and re-layouts  60 us (6%)
  other arithmetic  46.1 us (5%)
    pallas_call x6, Pallas kernels, assemble(): pl.pallas_call(assemble_kernel, out_shape=jax.ShapeDtypeStruct((4, 2, row...  457 us
    ppermute x36, waiting for transfers between devices, peer(): return lax.ppermute(value, 'fsdp', [(i, i ^ step) for i in range(4)])  71.8 us
    ppermute x18, waiting for transfers between devices, replica_sum(): lax.ppermute(value.astype(BF), 'replica', pairs).astype(F32)  52.7 us
    ppermute x36, starting transfers between devices, peer(): return lax.ppermute(value, 'fsdp', [(i, i ^ step) for i in range(4)])  45.5 us
    pallas_call x2, Pallas kernels, run_backward(): pl.pallas_call(attention_backward, out_shape=jax.ShapeDtypeStruct((tokens...  36.5 us
    dot_general x8, matrix products, dot(): return jnp.dot(a, b, preferred_element_type=F32)  32.2 us
    pallas_call x2, Pallas kernels, run_forward(): pl.pallas_call(attention_forward, out_shape=(shape((tokens, 576), BF), sh...  29 us
    dot_general x8, matrix products, dot_t(): lax.dot_general(a, b, (((1,), (1,)), ((), ())), preferred_element_type=F32)  26.9 us
  transfers between devices with their start and end apart: 92, of which 27 were waited for; matrix products, arithmetic and copies ran while one was open for 11% of the time, Pallas kernels for 41%

profile of v2, /device:TPU:0, one launch (start us, length us, event | category | flops | bytes accessed | tf_op | source)
XLA Modules:
  0.0 922.1 jit_solution(15784324245217468438)
XLA Ops:
  25.8 6.4 collective-permute-done.2.refs_2_
  40.5 5.4 collective-permute-done.18.refs_2_
  52.2 59.2 %assemble.6 = bf16[4,2,72,1664]{3,2,1,0:T(8,128)(2,1)} custom-call(bf16[72,1664]{1,0:T(8,128)(2,1)} %copy-done.37, bf16[72,1664]{1,0:T(8,128)(2,1)} %copy-done.63, bf16[72,1664]{1,0:T(8,128)(2,1)} %copy-done.64, bf16[72,1664]{1,0:T(8,128)(2,1)} %copy-done.65, bf16[72,1664]{1,0:T(8,128)(2,1)} %copy-done.68, bf16[72,1664]{1,0:T(8,128)(2,1)} %copy-done.71, ...), custom_call_target="tpu_custom_call" | custom-call | bytes 3833856 | tf_op jit(solution)/shard_map/assemble/pallas_call | solution.py:287
  119.9 14.7 %attention_forward.2 = (bf16[768,576]{1,0:T(8,128)(2,1)}, bf16[9,768,64]{2,1,0:T(8,128)(2,1)}, bf16[3,768,64]{2,1,0:T(8,128)(2,1)}, bf16[3,768,64]{2,1,0:T(8,128)(2,1)}, f32[9,1,768]{2,1,0:T(1,128)}) custom-call(f32[768,960]{1,0:T(8,128)} %fusion.33.qkv_ref, f32[768,128]{1,0:T(8,128)} %get-tuple-element.174.cos_ref, f32[768,128]{1,0:T(8,128)} %get-tuple-element.175.sin_ref, ...), custom_call_target="tpu_custom_call" | custom-call | flops 6000000000 | bytes 6000000 | tf_op jit(solution)/shard_map/attention_forward/pallas_call | solution.py:168
  144.6 60.8 %assemble.8 = bf16[4,2,192,576]{3,2,1,0:T(8,128)(2,1)} custom-call(bf16[192,576]{1,0:T(8,128)(2,1)} %copy-done.33, bf16[192,576]{1,0:T(8,128)(2,1)} %collective-permute-done.17.refs_1_, bf16[192,576]{1,0:T(8,128)(2,1)} %copy-done.50, bf16[192,576]{1,0:T(8,128)(2,1)} %copy-done.52, bf16[192,576]{1,0:T(8,128)(2,1)} %collective-permute-done.20.refs_4_, ...), custom_call_target="tpu_custom_call" | custom-call | bytes 3538944 | tf_op jit(solution)/shard_map/assemble/pallas_call | solution.py:287
  208.0 108.4 %assemble.7 = bf16[4,2,72,3072]{3,2,1,0:T(8,128)(2,1)} custom-call(bf16[72,3072]{1,0:T(8,128)(2,1)} %copy-done.25, bf16[72,3072]{1,0:T(8,128)(2,1)} %collective-permute-done.9.refs_1_, bf16[72,3072]{1,0:T(8,128)(2,1)} %collective-permute-done.10.refs_2_, bf16[72,3072]{1,0:T(8,128)(2,1)} %collective-permute-done.11.refs_3_, ...), custom_call_target="tpu_custom_call" | custom-call | bytes 7077888 | tf_op jit(solution)/shard_map/assemble/pallas_call | solution.py:287
  316.4 6.0 fusion.97
  333.1 59.2 %assemble.9 = bf16[4,2,72,1664]{3,2,1,0:T(8,128)(2,1)} custom-call(bf16[72,1664]{1,0:T(8,128)(2,1)} %copy-done.34, bf16[72,1664]{1,0:T(8,128)(2,1)} %copy-done.61, bf16[72,1664]{1,0:T(8,128)(2,1)} %collective-permute-done.25.refs_2_, bf16[72,1664]{1,0:T(8,128)(2,1)} %copy-done.66, bf16[72,1664]{1,0:T(8,128)(2,1)} %copy-done.67, bf16[72,1664]{1,0:T(8,128)(2,1)} %copy-done.69, ...), custom_call_target="tpu_custom_call" | custom-call | bytes 3833856 | tf_op jit(solution)/shard_map/assemble/pallas_call | solution.py:287
  400.1 14.3 %attention_forward.3 = (bf16[768,576]{1,0:T(8,128)(2,1)}, bf16[9,768,64]{2,1,0:T(8,128)(2,1)}, bf16[3,768,64]{2,1,0:T(8,128)(2,1)}, bf16[3,768,64]{2,1,0:T(8,128)(2,1)}, f32[9,1,768]{2,1,0:T(1,128)}) custom-call(f32[768,960]{1,0:T(8,128)} %fusion.29.qkv_ref, f32[768,128]{1,0:T(8,128)} %get-tuple-element.174.cos_ref, f32[768,128]{1,0:T(8,128)} %get-tuple-element.175.sin_ref, ...), custom_call_target="tpu_custom_call" | custom-call | flops 6000000000 | bytes 6000000 | tf_op jit(solution)/shard_map/attention_forward/pallas_call | solution.py:168
  422.0 60.7 %assemble.11 = bf16[4,2,192,576]{3,2,1,0:T(8,128)(2,1)} custom-call(bf16[192,576]{1,0:T(8,128)(2,1)} %copy-done.32, bf16[192,576]{1,0:T(8,128)(2,1)} %copy-done.54, bf16[192,576]{1,0:T(8,128)(2,1)} %collective-permute-done.39.refs_2_, bf16[192,576]{1,0:T(8,128)(2,1)} %copy-done.56, bf16[192,576]{1,0:T(8,128)(2,1)} %copy-done.58, ...), custom_call_target="tpu_custom_call" | custom-call | bytes 3538944 | tf_op jit(solution)/shard_map/assemble/pallas_call | solution.py:287
  483.5 108.4 %assemble.10 = bf16[4,2,72,3072]{3,2,1,0:T(8,128)(2,1)} custom-call(bf16[72,3072]{1,0:T(8,128)(2,1)} %copy-done.24, bf16[72,3072]{1,0:T(8,128)(2,1)} %collective-permute-done.31.refs_1_, bf16[72,3072]{1,0:T(8,128)(2,1)} %copy-done.46, bf16[72,3072]{1,0:T(8,128)(2,1)} %collective-permute-done.33.refs_3_, bf16[72,3072]{1,0:T(8,128)(2,1)} %collective-permute-done.34.refs_4_, ...), custom_call_target="tpu_custom_call" | custom-call | bytes 7077888 | tf_op jit(solution)/shard_map/assemble/pallas_call | solution.py:287
  591.9 6.1 fusion.98
  598.1 5.0 multiply_convert_fusion.3
  606.8 5.0 convolution_convert_fusion
  617.2 18.2 %attention_backward.2 = bf16[768,960]{1,0:T(8,128)(2,1)} custom-call(bf16[9,768,64]{2,1,0:T(8,128)(2,1)} %get-tuple-element.29.q_ref, bf16[3,768,64]{2,1,0:T(8,128)(2,1)} %get-tuple-element.30.k_ref, bf16[3,768,64]{2,1,0:T(8,128)(2,1)} %get-tuple-element.31.v_ref, f32[9,1,768]{2,1,0:T(1,128)} %get-tuple-element.32.lse_ref, ...), custom_call_target="tpu_custom_call" | custom-call | flops 12000000000 | bytes 7000000 | tf_op jit(solution)/shard_map/attention_backward/pallas_call | solution.py:191
  651.2 4.8 convolution_convert_fusion.1
  666.2 18.3 %attention_backward.3 = bf16[768,960]{1,0:T(8,128)(2,1)} custom-call(bf16[9,768,64]{2,1,0:T(8,128)(2,1)} %get-tuple-element.33.q_ref, bf16[3,768,64]{2,1,0:T(8,128)(2,1)} %get-tuple-element.34.k_ref, bf16[3,768,64]{2,1,0:T(8,128)(2,1)} %get-tuple-element.35.v_ref, f32[9,1,768]{2,1,0:T(1,128)} %get-tuple-element.36.lse_ref, ...), custom_call_target="tpu_custom_call" | custom-call | flops 12000000000 | bytes 7000000 | tf_op jit(solution)/shard_map/attention_backward/pallas_call | solution.py:191
  817.2 9.9 %collective-permute-done.90 = bf16[192,576]{1,0:T(8,128)(2,1)S(1)} collective-permute-done((bf16[192,576]{1,0:T(8,128)(2,1)S(1)}, bf16[192,576]{1,0:T(8,128)(2,1)S(1)}, u32[]{:S(2)}, u32[]{:S(2)}) %collective-permute-start.90) | collective-permute-done | bytes 221216 | tf_op jit(solution)/shard_map/ppermute | solution.py:334
  852.7 8.0 collective-permute-done.71
  864.0 5.5 collective-permute-done.63
  869.5 9.8 %collective-permute-done.64 = bf16[72,3072]{1,0:T(8,128)(2,1)} collective-permute-done((bf16[72,3072]{1,0:T(8,128)(2,1)}, bf16[72,3072]{1,0:T(8,128)(2,1)}, u32[]{:S(2)}, u32[]{:S(2)}) %collective-permute-start.64) | collective-permute-done | bytes 442400 | tf_op jit(solution)/shard_map/ppermute | solution.py:301
  883.0 8.5 collective-permute-done.66
  897.0 11.8 %collective-permute-done.75 = bf16[72,3072]{1,0:T(8,128)(2,1)S(1)} collective-permute-done((bf16[72,3072]{1,0:T(8,128)(2,1)S(1)}, bf16[72,3072]{1,0:T(8,128)(2,1)S(1)}, u32[]{:S(2)}, u32[]{:S(2)}) %collective-permute-start.75) | collective-permute-done | bytes 442400 | tf_op jit(solution)/shard_map/ppermute | solution.py:334
  908.8 8.8 collective-permute-done.68
  (487 shorter events, 296.1 us)
Async XLA Ops:
  47.8 70.9 %collective-permute-start.10 = (bf16[72,3072]{1,0:T(8,128)(2,1)S(1)}, bf16[72,3072]{1,0:T(8,128)(2,1)}, u32[]{:S(2)}, u32[]{:S(2)}) collective-permute-start(bf16[72,3072]{1,0:T(8,128)(2,1)S(1)} %get-tuple-element.126.refs_0_), channel_id=1, source_target_pairs={{0,8},{4,12},{8,0},{12,4},{1,9},{5,13},{9,1},{13,5},{2,10},{6,14},... | collective-permute-start | bytes 1327112 | tf_op jit(solution)/shard_map/ppermute | solution.py:301
  48.5 70.8 %collective-permute-start.11 = (bf16[72,3072]{1,0:T(8,128)(2,1)S(1)}, bf16[72,3072]{1,0:T(8,128)(2,1)}, u32[]{:S(2)}, u32[]{:S(2)}) collective-permute-start(bf16[72,3072]{1,0:T(8,128)(2,1)S(1)} %get-tuple-element.126.refs_0_), channel_id=1, source_target_pairs={{0,12},{4,8},{8,4},{12,0},{1,13},{5,9},{9,5},{13,1},{2,14},{6,10},... | collective-permute-start | bytes 1327112 | tf_op jit(solution)/shard_map/ppermute | solution.py:301
  50.0 69.4 %collective-permute-start.9 = (bf16[72,3072]{1,0:T(8,128)(2,1)S(1)}, bf16[72,3072]{1,0:T(8,128)(2,1)}, u32[]{:S(2)}, u32[]{:S(2)}) collective-permute-start(bf16[72,3072]{1,0:T(8,128)(2,1)S(1)} %get-tuple-element.126.refs_0_), channel_id=1, source_target_pairs={{0,4},{4,0},{8,12},{12,8},{1,5},{5,1},{9,13},{13,9},{2,6},{6,2},{1... | collective-permute-start | bytes 1327112 | tf_op jit(solution)/shard_map/ppermute | solution.py:301
  51.4 83.3 %collective-permute-start.20 = (bf16[192,576]{1,0:T(8,128)(2,1)S(1)}, bf16[192,576]{1,0:T(8,128)(2,1)}, u32[]{:S(2)}, u32[]{:S(2)}) collective-permute-start(bf16[192,576]{1,0:T(8,128)(2,1)S(1)} %get-tuple-element.24.refs_0_), channel_id=1, source_target_pairs={{0,16},{16,0},{1,17},{17,1},{2,18},{18,2},{3,19},{19,3},{4,20},{20... | collective-permute-start | bytes 663560 | tf_op jit(solution)/shard_map/ppermute | solution.py:305
  51.5 83.4 %collective-permute-start.21 = (bf16[192,576]{1,0:T(8,128)(2,1)}, bf16[192,576]{1,0:T(8,128)(2,1)}, u32[]{:S(2)}, u32[]{:S(2)}) collective-permute-start(bf16[192,576]{1,0:T(8,128)(2,1)} %collective-permute-done.17.refs_1_), channel_id=1, source_target_pairs={{0,16},{16,0},{1,17},{17,1},{2,18},{18,2},{3,19},{19,3},{4,20},{20... | collective-permute-start | bytes 663560 | tf_op jit(solution)/shard_map/ppermute | solution.py:305
  134.7 72.3 %collective-permute-start.12 = (bf16[72,3072]{1,0:T(8,128)(2,1)S(1)}, bf16[72,3072]{1,0:T(8,128)(2,1)}, u32[]{:S(2)}, u32[]{:S(2)}) collective-permute-start(bf16[72,3072]{1,0:T(8,128)(2,1)S(1)} %get-tuple-element.126.refs_0_), channel_id=1, source_target_pairs={{0,16},{16,0},{1,17},{17,1},{2,18},{18,2},{3,19},{19,3},{4,20},{20... | collective-permute-start | bytes 1327112 | tf_op jit(solution)/shard_map/ppermute | solution.py:305
  136.4 70.6 %collective-permute-start.13 = (bf16[72,3072]{1,0:T(8,128)(2,1)}, bf16[72,3072]{1,0:T(8,128)(2,1)}, u32[]{:S(2)}, u32[]{:S(2)}) collective-permute-start(bf16[72,3072]{1,0:T(8,128)(2,1)} %collective-permute-done.9.refs_1_), channel_id=1, source_target_pairs={{0,16},{16,0},{1,17},{17,1},{2,18},{18,2},{3,19},{19,3},{4,20},{20... | collective-permute-start | bytes 1327112 | tf_op jit(solution)/shard_map/ppermute | solution.py:305
  136.5 71.0 %collective-permute-start.14 = (bf16[72,3072]{1,0:T(8,128)(2,1)}, bf16[72,3072]{1,0:T(8,128)(2,1)}, u32[]{:S(2)}, u32[]{:S(2)}) collective-permute-start(bf16[72,3072]{1,0:T(8,128)(2,1)} %collective-permute-done.10.refs_2_), channel_id=1, source_target_pairs={{0,16},{16,0},{1,17},{17,1},{2,18},{18,2},{3,19},{19,3},{4,20},{20... | collective-permute-start | bytes 1327112 | tf_op jit(solution)/shard_map/ppermute | solution.py:305
  136.9 70.6 %collective-permute-start.15 = (bf16[72,3072]{1,0:T(8,128)(2,1)}, bf16[72,3072]{1,0:T(8,128)(2,1)}, u32[]{:S(2)}, u32[]{:S(2)}) collective-permute-start(bf16[72,3072]{1,0:T(8,128)(2,1)} %collective-permute-done.11.refs_3_), channel_id=1, source_target_pairs={{0,16},{16,0},{1,17},{17,1},{2,18},{18,2},{3,19},{19,3},{4,20},{20... | collective-permute-start | bytes 1327112 | tf_op jit(solution)/shard_map/ppermute | solution.py:305
  205.4 192.7 %collective-permute-start.31 = (bf16[72,3072]{1,0:T(8,128)(2,1)S(1)}, bf16[72,3072]{1,0:T(8,128)(2,1)}, u32[]{:S(2)}, u32[]{:S(2)}) collective-permute-start(bf16[72,3072]{1,0:T(8,128)(2,1)S(1)} %get-tuple-element.27.refs_0_), channel_id=1, source_target_pairs={{0,4},{4,0},{8,12},{12,8},{1,5},{5,1},{9,13},{13,9},{2,6},{6,2},{1... | collective-permute-start | bytes 1327112 | tf_op jit(solution)/shard_map/ppermute | solution.py:301
  206.9 121.8 %collective-permute-start.27 = (bf16[72,1664]{1,0:T(8,128)(2,1)S(1)}, bf16[72,1664]{1,0:T(8,128)(2,1)S(1)}, u32[]{:S(2)}, u32[]{:S(2)}) collective-permute-start(bf16[72,1664]{1,0:T(8,128)(2,1)S(1)} %get-tuple-element.25.refs_0_), channel_id=1, source_target_pairs={{0,16},{16,0},{1,17},{17,1},{2,18},{18,2},{3,19},{19,3},{4,20},{20... | collective-permute-start | bytes 718856 | tf_op jit(solution)/shard_map/ppermute | solution.py:305
  207.0 122.4 %collective-permute-start.28 = (bf16[72,1664]{1,0:T(8,128)(2,1)S(1)}, bf16[72,1664]{1,0:T(8,128)(2,1)S(1)}, u32[]{:S(2)}, u32[]{:S(2)}) collective-permute-start(bf16[72,1664]{1,0:T(8,128)(2,1)S(1)} %copy-done.62), channel_id=1, source_target_pairs={{0,16},{16,0},{1,17},{17,1},{2,18},{18,2},{3,19},{19,3},{4,20},{20... | collective-permute-start | bytes 718856 | tf_op jit(solution)/shard_map/ppermute | solution.py:305
  207.5 123.4 %collective-permute-start.29 = (bf16[72,1664]{1,0:T(8,128)(2,1)}, bf16[72,1664]{1,0:T(8,128)(2,1)S(1)}, u32[]{:S(2)}, u32[]{:S(2)}) collective-permute-start(bf16[72,1664]{1,0:T(8,128)(2,1)} %collective-permute-done.25.refs_2_), channel_id=1, source_target_pairs={{0,16},{16,0},{1,17},{17,1},{2,18},{18,2},{3,19},{19,3},{4,20},{20... | collective-permute-start | bytes 718856 | tf_op jit(solution)/shard_map/ppermute | solution.py:305
  207.6 124.8 %collective-permute-start.30 = (bf16[72,1664]{1,0:T(8,128)(2,1)S(1)}, bf16[72,1664]{1,0:T(8,128)(2,1)S(1)}, u32[]{:S(2)}, u32[]{:S(2)}) collective-permute-start(bf16[72,1664]{1,0:T(8,128)(2,1)S(1)} %collective-permute-done.26.refs_3_), channel_id=1, source_target_pairs={{0,16},{16,0},{1,17},{17,1},{2,18},{18,2},{3,19},{19,3},{4,20},{20... | collective-permute-start | bytes 718856 | tf_op jit(solution)/shard_map/ppermute | solution.py:305
  328.8 70.7 %collective-permute-start.32 = (bf16[72,3072]{1,0:T(8,128)(2,1)S(1)}, bf16[72,3072]{1,0:T(8,128)(2,1)S(1)}, u32[]{:S(2)}, u32[]{:S(2)}) collective-permute-start(bf16[72,3072]{1,0:T(8,128)(2,1)S(1)} %get-tuple-element.27.refs_0_), channel_id=1, source_target_pairs={{0,8},{4,12},{8,0},{12,4},{1,9},{5,13},{9,1},{13,5},{2,10},{6,14},... | collective-permute-start | bytes 1327112 | tf_op jit(solution)/shard_map/ppermute | solution.py:301
  329.4 84.9 %collective-permute-start.33 = (bf16[72,3072]{1,0:T(8,128)(2,1)S(1)}, bf16[72,3072]{1,0:T(8,128)(2,1)}, u32[]{:S(2)}, u32[]{:S(2)}) collective-permute-start(bf16[72,3072]{1,0:T(8,128)(2,1)S(1)} %get-tuple-element.27.refs_0_), channel_id=1, source_target_pairs={{0,12},{4,8},{8,4},{12,0},{1,13},{5,9},{9,5},{13,1},{2,14},{6,10},... | collective-permute-start | bytes 1327112 | tf_op jit(solution)/shard_map/ppermute | solution.py:301
  330.8 68.7 %collective-permute-start.38 = (bf16[192,576]{1,0:T(8,128)(2,1)S(1)}, bf16[192,576]{1,0:T(8,128)(2,1)S(1)}, u32[]{:S(2)}, u32[]{:S(2)}) collective-permute-start(bf16[192,576]{1,0:T(8,128)(2,1)S(1)} %get-tuple-element.28.refs_0_), channel_id=1, source_target_pairs={{0,4},{4,0},{8,12},{12,8},{1,5},{5,1},{9,13},{13,9},{2,6},{6,2},{1... | collective-permute-start | bytes 663560 | tf_op jit(solution)/shard_map/ppermute | solution.py:301
  332.4 82.2 %collective-permute-start.39 = (bf16[192,576]{1,0:T(8,128)(2,1)S(1)}, bf16[192,576]{1,0:T(8,128)(2,1)}, u32[]{:S(2)}, u32[]{:S(2)}) collective-permute-start(bf16[192,576]{1,0:T(8,128)(2,1)S(1)} %get-tuple-element.28.refs_0_), channel_id=1, source_target_pairs={{0,8},{4,12},{8,0},{12,4},{1,9},{5,13},{9,1},{13,5},{2,10},{6,14},... | collective-permute-start | bytes 663560 | tf_op jit(solution)/shard_map/ppermute | solution.py:301
  414.4 68.3 %collective-permute-start.34 = (bf16[72,3072]{1,0:T(8,128)(2,1)S(1)}, bf16[72,3072]{1,0:T(8,128)(2,1)}, u32[]{:S(2)}, u32[]{:S(2)}) collective-permute-start(bf16[72,3072]{1,0:T(8,128)(2,1)S(1)} %get-tuple-element.27.refs_0_), channel_id=1, source_target_pairs={{0,16},{16,0},{1,17},{17,1},{2,18},{18,2},{3,19},{19,3},{4,20},{20... | collective-permute-start | bytes 1327112 | tf_op jit(solution)/shard_map/ppermute | solution.py:305
  414.5 68.2 %collective-permute-start.35 = (bf16[72,3072]{1,0:T(8,128)(2,1)}, bf16[72,3072]{1,0:T(8,128)(2,1)}, u32[]{:S(2)}, u32[]{:S(2)}) collective-permute-start(bf16[72,3072]{1,0:T(8,128)(2,1)} %collective-permute-done.31.refs_1_), channel_id=1, source_target_pairs={{0,16},{16,0},{1,17},{17,1},{2,18},{18,2},{3,19},{19,3},{4,20},{20... | collective-permute-start | bytes 1327112 | tf_op jit(solution)/shard_map/ppermute | solution.py:305
  415.0 67.8 %collective-permute-start.36 = (bf16[72,3072]{1,0:T(8,128)(2,1)S(1)}, bf16[72,3072]{1,0:T(8,128)(2,1)}, u32[]{:S(2)}, u32[]{:S(2)}) collective-permute-start(bf16[72,3072]{1,0:T(8,128)(2,1)S(1)} %collective-permute-done.32.refs_2_), channel_id=1, source_target_pairs={{0,16},{16,0},{1,17},{17,1},{2,18},{18,2},{3,19},{19,3},{4,20},{20... | collective-permute-start | bytes 1327112 | tf_op jit(solution)/shard_map/ppermute | solution.py:305
  415.7 67.1 %collective-permute-start.37 = (bf16[72,3072]{1,0:T(8,128)(2,1)}, bf16[72,3072]{1,0:T(8,128)(2,1)S(1)}, u32[]{:S(2)}, u32[]{:S(2)}) collective-permute-start(bf16[72,3072]{1,0:T(8,128)(2,1)} %collective-permute-done.33.refs_3_), channel_id=1, source_target_pairs={{0,16},{16,0},{1,17},{17,1},{2,18},{18,2},{3,19},{19,3},{4,20},{20... | collective-permute-start | bytes 1327112 | tf_op jit(solution)/shard_map/ppermute | solution.py:305
  713.2 119.7 %collective-permute-start.69 = (bf16[4,72,3072]{2,1,0:T(8,128)(2,1)}, bf16[4,72,3072]{2,1,0:T(8,128)(2,1)}, u32[]{:S(2)}, u32[]{:S(2)}) collective-permute-start(bf16[4,72,3072]{2,1,0:T(8,128)(2,1)} %dynamic-slice_bitcast_fusion), channel_id=1, source_target_pairs={{0,16},{16,0},{1,17},{17,1},{2,18},{18,2},{3,19},{19,3},{4,20},{20... | collective-permute-start | bytes 5308424 | tf_op jit(solution)/shard_map/ppermute | solution.py:305
  737.4 100.4 %collective-permute-start.62 = (bf16[4,72,3072]{2,1,0:T(8,128)(2,1)S(1)}, bf16[4,72,3072]{2,1,0:T(8,128)(2,1)S(1)}, u32[]{:S(2)}, u32[]{:S(2)}) collective-permute-start(bf16[4,72,3072]{2,1,0:T(8,128)(2,1)S(1)} %dynamic-slice_bitcast_fusion.1), channel_id=1, source_target_pairs={{0,16},{16,0},{1,17},{17,1},{2,18},{18,2},{3,19},{19,3},{4,20},{20... | collective-permute-start | bytes 5308424 | tf_op jit(solution)/shard_map/ppermute | solution.py:305
  (156 other events, 3275.5 us)
